TPU v7x, 256 devices: a whole 4x4x8 slice. The times are simulated.
256 devices in a mesh: tile: 64 (over y, z_hi, x, core), plane: 4 (over z_lo).
Axes of the slice: x: 4, y: 4, z: 8 (z_hi: 2, z_lo: 4; z = z_hi * 4 + z_lo), core: 2. Of those that a mesh axis runs over, the one named last changes fastest.
Arguments:
- raw_tiles: bfloat16 [4, 512, 2, 16, 1024], P('plane', 'tile'), may hold values from 0.5 to 2.5
- flat_profile: bfloat16 [2, 16, 1024], P(None, 'plane'), may hold values from 0.5 to 1.5
- dark_profile: bfloat16 [2, 16, 1024], P(None, 'plane'), may hold values from 0 to 0.5
- destinations: int32 [4, 512, 1], P('plane', 'tile'), may hold values from 0 to 63, as said below
- positions: int32 [4, 512], P('plane', 'tile'), may hold values from 0 to 31
- levels: int32 [4, 512], P('plane', 'tile'), may hold values from 1 to 4
Outputs:
- stitched: bfloat16 [4, 2, 32768, 1024], P('plane', None, 'tile')
Inputs may be any that keep to these rules, and one draw needn't show every extreme that they name: `destinations`: the owner of a tile acquired by the device at index i of tile (aligned blocks of 8 tiles of a plane) is one of i - 2, ..., i + 2 or i + 32, modulo 64; among one device's tiles no owner is named more than 2 times, some owner exactly 2 times, and the owner i + 32 exactly 2 times.
All inputs are finite; a program needn't handle non-finite values.
Results may differ from a plain program's by a relative error of at most 0.0045.
Values may be sent and summed in bfloat16 or wider, within the bound.
A program may use at most 64 MiB of HBM per device.

v0:
```python
import jax
import jax.numpy as jnp
from jax import lax
from jax.sharding import PartitionSpec as P

CR = 512


screen_weight = 0.5


def padded(cells, sides, width):
    for axis, dim in sides:
        count = lax.axis_size(axis)
        ends = count - 1
        head = lax.slice_in_dim(cells, 0, width, axis=dim)
        tail = lax.slice_in_dim(cells, cells.shape[dim] - width, cells.shape[dim], axis=dim)
        cells = jnp.concatenate(
            [
                lax.ppermute(tail, axis, [(i, (i + 1) % count) for i in range(ends)]),
                cells,
                lax.ppermute(head, axis, [((i + 1) % count, i) for i in range(ends)]),
            ],
            axis=dim,
        )
    return cells


def ramp_weights(tile_rows):
    tile_row = jnp.arange(tile_rows)
    return jnp.minimum(tile_row + 1, tile_rows - tile_row).astype(jnp.float32)


def apply_weights(camera, flat_full, dark_full, gains):
    corrected = (
        camera.astype(jnp.float32) - dark_full.astype(jnp.float32)[None]
    ) / flat_full.astype(jnp.float32)[None]
    scale = gains[:, None, None, None] * ramp_weights(camera.shape[2])[None, None, :, None]
    return (corrected * scale).astype(jnp.bfloat16)


def neighbour_sum(above, below, middle):
    zero_col = jnp.zeros(middle.shape[:2] + (1,), jnp.float32)
    shifted_left = jnp.concatenate([zero_col, middle[:, :, :-1]], 2)
    shifted_right = jnp.concatenate([middle[:, :, 1:], zero_col], 2)
    return above + below + shifted_left + shifted_right


def per_device(raw_tiles, flat_profile, dark_profile, destinations, positions, levels):
    camera = raw_tiles[0]
    owners = destinations[0, :, 0]
    grid_pos = positions[0]
    gains_int = levels[0]
    tile_count = camera.shape[0]
    tile_rows = camera.shape[2]
    owner_count = lax.axis_size("tile")
    capacity = max(2, tile_count // 4)
    canvas_rows = CR
    flat_full, dark_full = (
        lax.all_gather(flat_profile, "plane", axis=1, tiled=True),
        lax.all_gather(dark_profile, "plane", axis=1, tiled=True),
    )
    same_dest = owners[:, None] == owners[None, :]
    earlier = jnp.arange(tile_count)[None, :] < jnp.arange(tile_count)[:, None]
    slot_rank = jnp.sum((same_dest & earlier).astype(jnp.int32), axis=1)
    slot_of = owners * capacity + slot_rank
    slot_total = owner_count * capacity
    matches = (slot_of[None, :] == jnp.arange(slot_total)[:, None]).astype(jnp.int32)
    slot_tile = jnp.sum(matches * jnp.arange(tile_count)[None, :], axis=1)
    occupied = jnp.sum(matches, axis=1)
    slot_gain = jnp.sum(matches * gains_int[None, :], axis=1)
    slot_pos = jnp.sum(matches * grid_pos[None, :], axis=1)
    slot_info = jnp.stack([slot_gain, slot_pos], 1).astype(jnp.bfloat16)
    occupied_mask = occupied.astype(jnp.bfloat16)[:, None, None, None]
    outgoing = jnp.take(camera, slot_tile, axis=0) * occupied_mask
    arrived, arrived_info = (
        lax.all_to_all(outgoing, "tile", split_axis=0, concat_axis=0, tiled=True),
        lax.all_to_all(slot_info, "tile", split_axis=0, concat_axis=0, tiled=True),
    )
    arrived_gain = arrived_info[:, 0].astype(jnp.float32)
    weighted = apply_weights(arrived, flat_full, dark_full, arrived_gain)
    first_rows = arrived_info[:, 1].astype(jnp.int32) * 16
    row_ids = jnp.arange(canvas_rows)[:, None, None]
    covered = row_ids == first_rows[None, :, None] + jnp.arange(tile_rows)[None, None, :]
    placement = covered.astype(jnp.bfloat16)
    accumulated = jnp.einsum(
        "ysr,scrx->cyx", placement, weighted, preferred_element_type=jnp.float32
    )
    row_gain = arrived_gain[:, None] * ramp_weights(tile_rows)[None, :]
    weight_sum = jnp.einsum("ysr,sr->y", covered.astype(jnp.float32), row_gain)
    blended = accumulated / jnp.maximum(weight_sum, 1.0)[None, :, None]
    field = blended
    for sweep_id in range(3):
        extended = padded(field, (("tile", 1),), 1)
        neighbours = neighbour_sum(extended[:, :-2], extended[:, 2:], field)
        field = (screen_weight * blended + neighbours) / (screen_weight + 4.0)
    return field.astype(jnp.bfloat16)[None]


def solution(mesh):
    placed = (
        P("plane", "tile", None, None, None),
        P(None, "plane", None),
        P(None, "plane", None),
        P("plane", "tile", None),
        P("plane", "tile"),
        P("plane", "tile"),
    )
    return jax.shard_map(
        per_device,
        mesh=mesh,
        in_specs=placed,
        out_specs=P("plane", None, "tile", None),
        check_vma=False,
    )
```

profile of v0, /device:TPU:15, one launch (start us, length us, event | category | flops | bytes accessed | tf_op | source)
XLA Modules:
  0.0 314.2 jit_solution(7593840456013712887)
XLA Ops:
  0.0 0.9 convert_reduce_fusion.1
  3.3 14.8 %all-to-all-start.1 = ((bf16[64,2,2]{1,2,0:T(2,128)(2,1)}), bf16[64,2,2]{1,2,0:T(2,128)(2,1)S(1)}, u32[]{:S(2)}, u32[]{:S(2)}) async-start(bf16[64,2,2]{1,2,0:T(2,128)(2,1)} %copy.27), calls=%async_computation.1 | async-start | bytes 65536 | tf_op jit(solution)/shard_map/all_to_all | solution.py:78
  18.2 6.2 %gather_fusion = bf16[128,2,16,1024]{3,2,1,0:T(8,128)(2,1)} fusion(bf16[8,2,16,1024]{3,2,1,0:T(8,128)(2,1)S(1)} %bitcast.36, s32[1024]{0:T(1024)S(1)} %pad_clamp_fusion), kind=kCustom, calls=%fused_computation | custom fusion | bytes 16777728 | tf_op jit(solution)/shard_map/jit(_take)/gather | solution.py:75
  24.5 7.5 %select_multiply_fusion = bf16[128,2,16,1024]{3,2,1,0:T(8,128)(2,1)} fusion(bf16[128,2,16,1024]{3,2,1,0:T(8,128)(2,1)} %gather_fusion, pred[128]{0:T(512)(128)(4,1)S(1)} %compare_and_fusion, bf16[128]{0:T(256)(128)(2,1)S(1)} %convert_element_type.65), kind=kLoop, calls=%fused_computation.2 | loop fusion | flops 8388608 | bytes 16777600 | tf_op jit(solution)/shard_map/mul | solution.py:75
  32.0 13.1 %all-to-all-start = ((bf16[128,2,16,1024]{3,2,1,0:T(8,128)(2,1)}), bf16[128,2,16,1024]{3,2,1,0:T(8,128)(2,1)}, u32[]{:S(2)}, u32[]{:S(2)}) async-start(bf16[128,2,16,1024]{3,2,1,0:T(8,128)(2,1)} %select_multiply_fusion), calls=%async_computation | async-start | bytes 16777216 | tf_op jit(solution)/shard_map/all_to_all | solution.py:77
  45.1 191.3 %all_gather.6 = bf16[2,16,1024]{2,0,1:T(2,128)(2,1)S(1)} all-gather(bf16[2,4,1024]{2,0,1:T(2,128)(2,1)S(1)} %copy.23), channel_id=1, replica_groups=mesh['tile'=64,'plane'=4] {'plane'}, dimensions={1}, use_global_device_ids=true | all-gather | bytes 81920 | tf_op jit(solution)/shard_map/all_gather | solution.py:61
  236.4 10.3 %all_gather.7 = bf16[2,16,1024]{2,0,1:T(2,128)(2,1)S(1)} all-gather(bf16[2,4,1024]{2,0,1:T(2,128)(2,1)S(1)} %copy.25), channel_id=1, replica_groups=mesh['tile'=64,'plane'=4] {'plane'}, dimensions={1}, use_global_device_ids=true | all-gather | bytes 81920 | tf_op jit(solution)/shard_map/all_gather | solution.py:60
  247.1 0.8 fusion.18
  247.9 9.2 %fusion.17 = f32[2,512,1024]{2,1,0:T(8,128)S(1)} fusion(f32[512]{0:T(512)S(1)} %broadcast_maximum_fusion, s32[128,16]{1,0:T(8,128)S(1)} %iota_add_fusion, bf16[128,2,16,1024]{3,2,1,0:T(8,128)(2,1)} %all-to-all-done, f32[128,16]{1,0:T(8,128)S(1)} %broadcast_multiply_fusion, f32[2,16,1024]{2,1,0:T(8,128)S(1)} %copy_convert_fusion, ...), kind=kOutput, calls=%fused_computation.27 | convolution fusion | flops 4318035968 | bytes 12863488 | tf_op jit(solution)/shard_map/ysr,scrx->cyx/dot_general | solution.py:86
  257.1 9.6 %collective-permute-start = (f32[2,1,1024]{2,1,0:T(1,128)S(1)}, f32[2,1,1024]{2,1,0:T(1,128)S(1)}, u32[]{:S(2)}, u32[]{:S(2)}) collective-permute-start(f32[2,1,1024]{2,1,0:T(1,128)S(1)} %get-tuple-element.19), channel_id=1, source_target_pairs={{0,4},{4,8},{8,12},{12,16},{16,20},{20,24},{24,28},{28,32},{32,36}... | collective-permute-start | bytes 24584 | tf_op jit(solution)/shard_map/ppermute | solution.py:20
  266.7 2.1 collective-permute-start.1
  268.8 1.7 fusion.34
  270.5 7.2 %collective-permute-done.1 = f32[2,1,1024]{2,1,0:T(1,128)S(1)} collective-permute-done((f32[2,1,1024]{2,1,0:T(1,128)S(1)}, f32[2,1,1024]{2,1,0:T(1,128)S(1)}, u32[]{:S(2)}, u32[]{:S(2)}) %collective-permute-start.1) | collective-permute-done | bytes 8224 | tf_op jit(solution)/shard_map/ppermute | solution.py:22
  277.7 2.7 fusion.16
  280.4 2.5 collective-permute-start.2
  282.9 1.9 collective-permute-start.3
  284.8 1.7 fusion.32
  286.5 7.4 %collective-permute-done.3 = f32[2,1,1024]{2,1,0:T(1,128)S(1)} collective-permute-done((f32[2,1,1024]{2,1,0:T(1,128)S(1)}, f32[2,1,1024]{2,1,0:T(1,128)S(1)}, u32[]{:S(2)}, u32[]{:S(2)}) %collective-permute-start.3) | collective-permute-done | bytes 8224 | tf_op jit(solution)/shard_map/ppermute | solution.py:22
  293.9 3.1 fusion.11
  297.0 2.3 collective-permute-start.4
  299.3 2.0 collective-permute-start.5
  301.3 1.7 fusion.31
  303.0 7.3 %collective-permute-done.5 = f32[2,1,1024]{2,1,0:T(1,128)S(1)} collective-permute-done((f32[2,1,1024]{2,1,0:T(1,128)S(1)}, f32[2,1,1024]{2,1,0:T(1,128)S(1)}, u32[]{:S(2)}, u32[]{:S(2)}) %collective-permute-start.5) | collective-permute-done | bytes 8224 | tf_op jit(solution)/shard_map/ppermute | solution.py:22
  310.3 3.9 %fusion.23 = bf16[1,2,512,1024]{3,2,1,0:T(8,128)(2,1)} fusion(f32[2,512,1023]{2,1,0:T(8,128)S(1)} %get-tuple-element.12, f32[2,512,1023]{2,1,0:T(8,128)S(1)} %get-tuple-element.11, f32[2,1,1024]{2,1,0:T(1,128)S(1)} %collective-permute-done.5, f32[2,512,1024]{2,1,0:T(8,128)S(1)} %fusion.11, f32[2,1,1024]{2,1,0:T(1,128)S(1)} %collective-permute-done.4, ...), kind=kLoop, calls=%fused_computation.33 | loop fusion | flops 9437184 | bytes 18882560 | tf_op jit(solution)/shard_map/broadcast_in_dim | solution.py:97
  (38 shorter events, 2.9 us)
Async XLA Ops:
  0.0 18.2 %copy-start = (bf16[1,8,2,16,1024]{4,3,2,1,0:T(8,128)(2,1)S(1)}, bf16[1,8,2,16,1024]{4,3,2,1,0:T(8,128)(2,1)}, u32[]{:S(2)}) copy-start(bf16[1,8,2,16,1024]{4,3,2,1,0:T(8,128)(2,1)} %param.6) | copy-start | bytes 1572868
  3.3 28.6 %all-to-all-start.1 = ((bf16[64,2,2]{1,2,0:T(2,128)(2,1)}), bf16[64,2,2]{1,2,0:T(2,128)(2,1)S(1)}, u32[]{:S(2)}, u32[]{:S(2)}) async-start(bf16[64,2,2]{1,2,0:T(2,128)(2,1)} %copy.27), calls=%async_computation.1 | async-start | bytes 65536 | tf_op jit(solution)/shard_map/all_to_all | solution.py:78
  32.0 13.1 %copy-start.1 = (bf16[2,4,1024]{2,1,0:T(4,128)(2,1)S(1)}, bf16[2,4,1024]{2,1,0:T(4,128)(2,1)}, u32[]{:S(2)}) copy-start(bf16[2,4,1024]{2,1,0:T(4,128)(2,1)} %param.7) | copy-start | bytes 49156
  32.0 13.1 %copy-start.2 = (bf16[2,4,1024]{2,1,0:T(4,128)(2,1)S(1)}, bf16[2,4,1024]{2,1,0:T(4,128)(2,1)}, u32[]{:S(2)}) copy-start(bf16[2,4,1024]{2,1,0:T(4,128)(2,1)} %param.8) | copy-start | bytes 49156
  32.0 216.0 %all-to-all-start = ((bf16[128,2,16,1024]{3,2,1,0:T(8,128)(2,1)}), bf16[128,2,16,1024]{3,2,1,0:T(8,128)(2,1)}, u32[]{:S(2)}, u32[]{:S(2)}) async-start(bf16[128,2,16,1024]{3,2,1,0:T(8,128)(2,1)} %select_multiply_fusion), calls=%async_computation | async-start | bytes 16777216 | tf_op jit(solution)/shard_map/all_to_all | solution.py:77
  257.1 13.4 %collective-permute-start = (f32[2,1,1024]{2,1,0:T(1,128)S(1)}, f32[2,1,1024]{2,1,0:T(1,128)S(1)}, u32[]{:S(2)}, u32[]{:S(2)}) collective-permute-start(f32[2,1,1024]{2,1,0:T(1,128)S(1)} %get-tuple-element.19), channel_id=1, source_target_pairs={{0,4},{4,8},{8,12},{12,16},{16,20},{20,24},{24,28},{28,32},{32,36}... | collective-permute-start | bytes 24584 | tf_op jit(solution)/shard_map/ppermute | solution.py:20
  266.7 11.0 %collective-permute-start.1 = (f32[2,1,1024]{2,1,0:T(1,128)S(1)}, f32[2,1,1024]{2,1,0:T(1,128)S(1)}, u32[]{:S(2)}, u32[]{:S(2)}) collective-permute-start(f32[2,1,1024]{2,1,0:T(1,128)S(1)} %get-tuple-element.20), channel_id=1, source_target_pairs={{4,0},{8,4},{12,8},{16,12},{20,16},{24,20},{28,24},{32,28},{36,32}... | collective-permute-start | bytes 24584 | tf_op jit(solution)/shard_map/ppermute | solution.py:22
  280.4 6.1 %collective-permute-start.2 = (f32[2,1,1024]{2,1,0:T(1,128)S(1)}, f32[2,1,1024]{2,1,0:T(1,128)S(1)}, u32[]{:S(2)}, u32[]{:S(2)}) collective-permute-start(f32[2,1,1024]{2,1,0:T(1,128)S(1)} %get-tuple-element.15), channel_id=1, source_target_pairs={{0,4},{4,8},{8,12},{12,16},{16,20},{20,24},{24,28},{28,32},{32,36}... | collective-permute-start | bytes 24584 | tf_op jit(solution)/shard_map/ppermute | solution.py:20
  282.9 11.0 %collective-permute-start.3 = (f32[2,1,1024]{2,1,0:T(1,128)S(1)}, f32[2,1,1024]{2,1,0:T(1,128)S(1)}, u32[]{:S(2)}, u32[]{:S(2)}) collective-permute-start(f32[2,1,1024]{2,1,0:T(1,128)S(1)} %get-tuple-element.16), channel_id=1, source_target_pairs={{4,0},{8,4},{12,8},{16,12},{20,16},{24,20},{28,24},{32,28},{36,32}... | collective-permute-start | bytes 24584 | tf_op jit(solution)/shard_map/ppermute | solution.py:22
  297.0 6.0 %collective-permute-start.4 = (f32[2,1,1024]{2,1,0:T(1,128)S(1)}, f32[2,1,1024]{2,1,0:T(1,128)S(1)}, u32[]{:S(2)}, u32[]{:S(2)}) collective-permute-start(f32[2,1,1024]{2,1,0:T(1,128)S(1)} %get-tuple-element.9), channel_id=1, source_target_pairs={{0,4},{4,8},{8,12},{12,16},{16,20},{20,24},{24,28},{28,32},{32,36}... | collective-permute-start | bytes 24584 | tf_op jit(solution)/shard_map/ppermute | solution.py:20
  299.3 11.0 %collective-permute-start.5 = (f32[2,1,1024]{2,1,0:T(1,128)S(1)}, f32[2,1,1024]{2,1,0:T(1,128)S(1)}, u32[]{:S(2)}, u32[]{:S(2)}) collective-permute-start(f32[2,1,1024]{2,1,0:T(1,128)S(1)} %get-tuple-element.10), channel_id=1, source_target_pairs={{4,0},{8,4},{12,8},{16,12},{20,16},{24,20},{28,24},{32,28},{36,32}... | collective-permute-start | bytes 24584 | tf_op jit(solution)/shard_map/ppermute | solution.py:22
where the time goes:
time: 315 us; the launch traced here: 314 us
  blocking collectives  202 us (64%)
  starting transfers between devices  48.3 us (15%)
  waiting for transfers between devices  21.9 us (7%)
  other arithmetic  19.7 us (6%)
  local copies, waits for them, and re-layouts  12.4 us (4%)
  matrix products  10 us (3%)
    all_gather x1, blocking collectives, per_device(): lax.all_gather(dark_profile, 'plane', axis=1, tiled=True)  191 us
    ppermute x3, waiting for transfers between devices, padded(): lax.ppermute(head, axis, [((i + 1) % count, i) for i in range(ends)])  21.9 us
    all_to_all x1, starting transfers between devices, per_device(): lax.all_to_all(slot_info, 'tile', split_axis=0, concat_axis=0, tiled=True)  14.8 us
    ppermute x3, starting transfers between devices, padded(): lax.ppermute(tail, axis, [(i, (i + 1) % count) for i in range(ends)])  14.4 us
    all_to_all x1, starting transfers between devices, per_device(): lax.all_to_all(outgoing, 'tile', split_axis=0, concat_axis=0, tiled=True)  13.1 us
    all_gather x1, blocking collectives, per_device(): lax.all_gather(flat_profile, 'plane', axis=1, tiled=True)  10.3 us
    dot_general x1, matrix products, per_device(): jnp.einsum('ysr,scrx->cyx', placement, weighted, preferred_element_type=j...  9.17 us
    mul x1, other arithmetic, per_device(): outgoing = jnp.take(camera, slot_tile, axis=0) * occupied_mask  7.48 us
  transfers between devices with their start and end apart: 8, of which 3 were waited for; matrix products, arithmetic and copies ran while one was open for 6% of the time, Pallas kernels for 0%

commit v1 on v0

v1 whole, which is shorter than its diff:
```python
import functools

import jax
import jax.numpy as jnp
from jax import lax
from jax.experimental import pallas as pl
from jax.experimental.pallas import tpu as pltpu
from jax.sharding import PartitionSpec as P

MESH = pl.DeviceIdType.MESH
F32 = jnp.float32
BF16 = jnp.bfloat16
OWNER_ROWS = 512
TILE_ROWS = 16
NEAR = (-2, -1, 1, 2)
GROUPS = 7
DEPTH = GROUPS * 128
Q = 1.0 / 4.5
Q2 = Q * Q
Q3 = Q2 * Q


def stitch_kernel(
    n_tile, n_plane, width,
    dest_ref, pos_ref, level_ref, raw_ref, flat_ref, dark_ref, out_ref,
    rawv, sbuf, rbuf, smeta, rmeta, prof, dark_v, inv_v, pos_all, gain_all, g_all,
    edge, strip, sblk, rblk, sstrip, rstrip, vbuf, mbuf, obuf,
    raw_sem, own_sem, out_sem,
    tile_s, tile_r, meta_s, meta_r, gat_s, gat_r, swap_s, swap_r, blk_s, blk_r, str_s, str_r,
):
    me = lax.axis_index("tile")
    plane = lax.axis_index("plane")
    core = lax.rem(me, 2)
    column = lax.rem(me // 2, 4)
    up = column >= 2
    half = n_tile // 2
    reps = width // 128

    def at(offset):
        return {"tile": lax.rem(me + offset + n_tile, n_tile), "plane": plane}

    load_raw = pltpu.make_async_copy(raw_ref.at[0], rawv, raw_sem)
    load_raw.start()

    @pl.when(core == 0)
    def _():
        pltpu.make_async_copy(flat_ref, prof.at[0, plane], own_sem).start()

    @pl.when(core == 1)
    def _():
        pltpu.make_async_copy(dark_ref, prof.at[1, plane], own_sem).start()

    barrier = pltpu.get_barrier_semaphore()
    for offset in NEAR + (half,):
        pl.semaphore_signal(barrier, inc=1, device_id=at(offset), device_id_type=MESH)
    for k in range(1, n_plane):
        mate = {"tile": me, "plane": lax.rem(plane + k, n_plane)}
        pl.semaphore_signal(barrier, inc=1, device_id=mate, device_id_type=MESH)

    rel = [lax.rem(dest_ref[0, t, 0] - me + 2 + 2 * n_tile, n_tile) for t in range(8)]
    load_raw.wait()
    for e, offset in enumerate(NEAR + (half, 0)):
        key = offset + 2
        first, last, hits = jnp.int32(0), jnp.int32(0), jnp.int32(0)
        for t in range(8):
            hit = rel[t] == key
            last = jnp.where(hit, t, last)
            hits = hits + jnp.where(hit, 1, 0)
            first = jnp.where(rel[7 - t] == key, 7 - t, first)
        gain0 = jnp.where(hits > 0, level_ref[0, first], 0).astype(F32)
        gain1 = jnp.where(hits > 1, level_ref[0, last], 0).astype(F32)
        pos0 = pos_ref[0, first].astype(F32)
        pos1 = pos_ref[0, last].astype(F32)
        row = lax.broadcasted_iota(jnp.int32, (8, 128), 0)
        meta = jnp.where(row == 0, pos0, jnp.where(row == 1, pos1, jnp.where(row == 2, gain0, gain1)))
        smeta[e] = meta
        if e == 5:
            rmeta[5] = meta
            rbuf[5, 0] = rawv[first]
            rbuf[5, 1] = rawv[last]
        else:
            sbuf[e, 0] = rawv[first]
            sbuf[e, 1] = rawv[last]

    def profile_wait_own():
        pltpu.make_async_copy(flat_ref, prof.at[core, plane], own_sem).wait()

    profile_wait_own()
    pl.semaphore_wait(barrier, 4 + n_plane)

    sends = []

    def send(src, dst, s_sem, r_sem, device):
        copy = pltpu.make_async_remote_copy(src, dst, s_sem, r_sem, device_id=device, device_id_type=MESH)
        copy.start()
        sends.append(copy)

    def slot_at_target(e):
        return 3 - e if e < 4 else 4

    for e, offset in enumerate(NEAR + (half,)):
        f = slot_at_target(e)
        send(smeta.at[e], rmeta.at[f], meta_s.at[e], meta_r.at[f], at(offset))
    for j in range(2):
        e = jnp.where(up, 3 - j, j)
        offset = jnp.where(up, 2 - j, j - 2)
        for k in range(2):
            send(sbuf.at[e, k], rbuf.at[3 - e, k], tile_s.at[e, k], tile_r.at[3 - e, k], at(offset))
    for k in range(1, n_plane):
        mate = {"tile": me, "plane": lax.rem(plane + k, n_plane)}
        send(prof.at[core, plane], prof.at[core, plane], gat_s.at[k], gat_r.at[plane], mate)
    for k in range(2):
        send(sbuf.at[4, k], rbuf.at[4, k], tile_s.at[4, k], tile_r.at[4, k], at(half))
    for j in range(2):
        e = jnp.where(up, j, 3 - j)
        offset = jnp.where(up, j - 2, 2 - j)
        for k in range(2):
            send(sbuf.at[e, k], rbuf.at[3 - e, k], tile_s.at[e, k], tile_r.at[3 - e, k], at(offset))

    for k in range(1, n_plane):
        source = lax.rem(plane + k, n_plane)
        pltpu.make_async_remote_copy(
            prof.at[core, source], prof.at[core, source], gat_s.at[k], gat_r.at[source],
            device_id=at(1), device_id_type=MESH,
        ).wait_recv()
    other = {"tile": me + 1 - 2 * core, "plane": plane}
    send(prof.at[core], prof.at[core], swap_s, swap_r, other)
    pltpu.make_async_remote_copy(
        prof.at[1 - core], prof.at[1 - core], swap_s, swap_r, device_id=other, device_id_type=MESH
    ).wait_recv()
    part = TILE_ROWS // n_plane
    for p in range(n_plane):
        inv_v[:, p * part:(p + 1) * part, :] = 1.0 / prof[0, p].astype(F32)
        dark_v[:, p * part:(p + 1) * part, :] = prof[1, p].astype(F32)

    row16 = lax.broadcasted_iota(jnp.int32, (TILE_ROWS, 128), 0)
    ramp = jnp.minimum(row16 + 1, TILE_ROWS - row16).astype(F32)

    def wide(x):
        return jnp.concatenate([x] * reps, axis=1)

    for e in range(4):
        lo, at_pos = (8, 31.0) if e < 2 else (0, 0.0)
        for ch in range(2):
            total = None
            for k in range(2):
                keep = jnp.where(smeta[e, k:k + 1, :] == at_pos, 1.0, 0.0)
                scale = wide(ramp[lo:lo + 8] * smeta[e, 2 + k:3 + k, :])
                tile = sbuf[e, k, ch].astype(F32)[lo:lo + 8]
                w = (tile - dark_v[ch, lo:lo + 8]) * inv_v[ch, lo:lo + 8] * scale
                w = w.astype(BF16).astype(F32) * wide(jnp.broadcast_to(keep, (8, 128)))
                total = w if total is None else total + w
            strip[e, ch] = total
    for j, (e, offset) in enumerate(((0, -1), (3, 1))):
        sstrip[j] = jnp.concatenate([strip[e, 0], strip[e, 1]], axis=0).astype(BF16)
        send(sstrip.at[j], rstrip.at[1 - j], str_s.at[j], str_r.at[1 - j], at(offset))

    order = (5, 4) + tuple(jnp.where(up, a, 3 - a) for a in (1, 0, 2, 3))
    for f in range(5):
        pltpu.make_async_remote_copy(
            smeta.at[f], rmeta.at[f], meta_s.at[f], meta_r.at[f], device_id=at(1), device_id_type=MESH
        ).wait_recv()
    pos_all[...] = jnp.full((16, 128), -99.0, F32)
    gain_all[...] = jnp.zeros((16, 128), F32)
    for m in range(6):
        pos_all[2 * m:2 * m + 2] = rmeta[order[m], 0:2]
        gain_all[2 * m:2 * m + 2] = rmeta[order[m], 2:4]
    positions, gains = pos_all[...], gain_all[...]

    def gain_sum(p):
        return jnp.sum(jnp.where(positions == p, gains, 0.0), axis=0, keepdims=True)

    for j in range(12):
        g_all[j:j + 1] = gain_sum(positions[j:j + 1])
    gain_first, gain_last = gain_sum(0.0), gain_sum(31.0)

    lane = lax.broadcasted_iota(jnp.int32, (1, 128), 1)
    gap = lax.rem(lane // TILE_ROWS, 4).astype(F32)
    y = lax.broadcasted_iota(jnp.int32, (OWNER_ROWS, 128), 0).astype(F32)
    top_shift = jnp.where(me == 0, 2.0, 1e6).astype(F32)
    bottom_shift = jnp.where(me == n_tile - 1, -2.0 * OWNER_ROWS, 1e6).astype(F32)
    for m in range(GROUPS):
        if m < 6:
            p0, p1 = positions[2 * m:2 * m + 1], positions[2 * m + 1:2 * m + 2]
        else:
            p0, p1 = -1.0, float(OWNER_ROWS // TILE_ROWS)
        source_row = jnp.where(lane < 64, p0, p1) * TILE_ROWS + lax.rem(lane, TILE_ROWS).astype(F32)
        hit = jnp.where(jnp.abs(y - source_row) == gap, 1.0, 0.0)
        above = jnp.where(jnp.abs(y + source_row + top_shift) == gap, 1.0, 0.0)
        below = jnp.where(jnp.abs(y + source_row + bottom_shift) == gap, 1.0, 0.0)
        mbuf[:, m * 128:(m + 1) * 128] = (hit - above - below).astype(BF16)

    col = lax.broadcasted_iota(jnp.int32, (TILE_ROWS, width), 1)
    not_first, not_last = col > 0, col < width - 1

    def sides(x):
        return jnp.where(not_first, pltpu.roll(x, 1, 1), 0.0) + jnp.where(
            not_last, pltpu.roll(x, width - 1, 1), 0.0
        )

    def spread(m, k, ch, b):
        c1 = sides(b)
        c2 = sides(c1)
        c3 = sides(c2)
        two = (0.5 * Q3) * b + (3.0 * Q3) * c1
        zero = (0.5 * Q) * b + (0.5 * Q2) * c1 + (0.5 * Q3) * c2 + Q3 * c3 + 2.0 * two
        one = (0.5 * Q2 + 3.0 * Q3) * b + Q3 * c1 + (3.0 * Q3) * c2
        base = m * 128 + k * 64
        for d, v in enumerate((zero, one, two, Q3 * b)):
            start = base + d * TILE_ROWS
            if not isinstance(start, int):
                start = pl.multiple_of(start, TILE_ROWS)
            vbuf[ch, pl.ds(start, TILE_ROWS), :] = v.astype(BF16)

    edge[...] = jnp.zeros(edge.shape, F32)
    last_row = jnp.where(up, 31.0, 0.0).astype(F32)
    other_row = jnp.where(up, 0.0, 31.0).astype(F32)

    def work(m):
        e = order[m]
        if m > 0:
            for k in range(2):
                pltpu.make_async_remote_copy(
                    sbuf.at[0, k], rbuf.at[e, k], tile_s.at[0, k], tile_r.at[e, k],
                    device_id=at(1), device_id_type=MESH,
                ).wait_recv()

        def unit(u, carry):
            k, ch = u // 2, lax.rem(u, 2)
            gain = gain_all[pl.ds(2 * m + k, 1), :]
            p = pos_all[pl.ds(2 * m + k, 1), :]
            g = g_all[pl.ds(2 * m + k, 1), :]
            w = (rbuf[e, k, ch].astype(F32) - dark_v[ch]) * inv_v[ch] * wide(ramp * gain)
            w = w.astype(BF16).astype(F32)
            lower, upper = w[0:8], w[8:16]
            if m < 4:
                keep = wide(jnp.broadcast_to(jnp.where(p == last_row, 1.0, 0.0), (8, 128)))
                edge[0, ch] += keep * jnp.where(up, upper, lower)
            if m < 2 or m >= 4:
                keep = wide(jnp.broadcast_to(jnp.where(p == other_row, 1.0, 0.0), (8, 128)))
                edge[1, ch] += keep * jnp.where(up, lower, upper)
            spread(m, k, ch, w * wide(1.0 / jnp.maximum(ramp * g, 1.0)))
            return carry

        lax.fori_loop(0, 4, unit, 0)

    def send_edge(j):
        down = up if j == 0 else jnp.logical_not(up)
        total = jnp.where(down, gain_last, gain_first)
        mark = lax.broadcasted_iota(jnp.int32, (8, width), 0) == 4
        block = [jnp.where(mark, wide(jnp.broadcast_to(total, (8, 128))), edge[j, ch]) for ch in range(2)]
        sblk[j] = jnp.concatenate(block, axis=0).astype(BF16)
        offset = jnp.where(down, 1, -1)
        lands = jnp.where(down, 0, 1)
        send(sblk.at[j], rblk.at[lands], blk_s.at[j], blk_r.at[lands], at(offset))

    for m in range(4):
        work(m)
    send_edge(0)
    for m in range(4, 6):
        work(m)
    send_edge(1)

    for j in range(2):
        pltpu.make_async_remote_copy(
            sstrip.at[j], rstrip.at[j], str_s.at[j], str_r.at[j], device_id=at(1), device_id_type=MESH
        ).wait_recv()
        pltpu.make_async_remote_copy(
            sblk.at[j], rblk.at[j], blk_s.at[j], blk_r.at[j], device_id=at(1), device_id_type=MESH
        ).wait_recv()
    for j in range(2):
        inside = jnp.where(me == (0 if j == 0 else n_tile - 1), 0.0, 1.0).astype(F32)
        lo = 8 - 8 * j
        got, direct = rblk[j].astype(F32), rstrip[1 - j].astype(F32)
        weights = jnp.broadcast_to(got[4:5], (8, width)) * wide(ramp[lo:lo + 8])
        scale = inside / jnp.maximum(weights, 1.0)
        for ch in range(2):
            rows = (got[8 * ch:8 * ch + 8] + direct[8 * ch:8 * ch + 8] + strip[1 + j, ch]) * scale
            none = jnp.zeros((8, width), F32)
            spread(6, j, ch, jnp.concatenate([none, rows] if j == 0 else [rows, none], axis=0))

    span = 256

    def block(n, carry):
        ch, start = n // (width // span), pl.multiple_of(lax.rem(n, width // span) * span, span)
        made = jnp.dot(mbuf[...], vbuf[ch, :, pl.ds(start, span)], preferred_element_type=F32)
        obuf[ch, :, pl.ds(start, span)] = made.astype(BF16)
        pltpu.make_async_copy(
            obuf.at[ch, :, pl.ds(start, span)], out_ref.at[0, ch, :, pl.ds(start, span)], out_sem.at[n]
        ).start()
        return carry

    blocks = 2 * width // span
    lax.fori_loop(0, blocks, block, 0)
    for n in range(blocks):
        ch, start = n // (width // span), n % (width // span) * span
        pltpu.make_async_copy(
            obuf.at[ch, :, pl.ds(start, span)], out_ref.at[0, ch, :, pl.ds(start, span)], out_sem.at[n]
        ).wait()
    for copy in sends:
        copy.wait_send()


def solution(mesh):
    n_tile, n_plane = mesh.shape["tile"], mesh.shape["plane"]

    def per_device(raw_tiles, flat_profile, dark_profile, destinations, positions, levels):
        width = raw_tiles.shape[-1]
        tile = (2, TILE_ROWS, width)
        dma = pltpu.SemaphoreType.DMA
        return pl.pallas_call(
            functools.partial(stitch_kernel, n_tile, n_plane, width),
            out_shape=jax.ShapeDtypeStruct((1, 2, OWNER_ROWS, width), BF16),
            in_specs=[pl.BlockSpec(memory_space=pltpu.SMEM)] * 3 + [pl.BlockSpec(memory_space=pl.ANY)] * 3,
            out_specs=pl.BlockSpec(memory_space=pl.ANY),
            scratch_shapes=[
                pltpu.VMEM((8,) + tile, BF16),
                pltpu.VMEM((5, 2) + tile, BF16),
                pltpu.VMEM((6, 2) + tile, BF16),
                pltpu.VMEM((6, 8, 128), F32),
                pltpu.VMEM((6, 8, 128), F32),
                pltpu.VMEM((2, n_plane, 2, TILE_ROWS // n_plane, width), BF16),
                pltpu.VMEM(tile, F32),
                pltpu.VMEM(tile, F32),
                pltpu.VMEM((16, 128), F32),
                pltpu.VMEM((16, 128), F32),
                pltpu.VMEM((16, 128), F32),
                pltpu.VMEM((2, 2, 8, width), F32),
                pltpu.VMEM((4, 2, 8, width), F32),
                pltpu.VMEM((2, 16, width), BF16),
                pltpu.VMEM((2, 16, width), BF16),
                pltpu.VMEM((2, 16, width), BF16),
                pltpu.VMEM((2, 16, width), BF16),
                pltpu.VMEM((2, DEPTH, width), BF16),
                pltpu.VMEM((OWNER_ROWS, DEPTH), BF16),
                pltpu.VMEM((2, OWNER_ROWS, width), BF16),
                dma, dma, dma((2 * width // 256,)),
                dma((5, 2)), dma((5, 2)), dma((5,)), dma((5,)),
                dma((n_plane,)), dma((n_plane,)), dma, dma,
                dma((2,)), dma((2,)), dma((2,)), dma((2,)),
            ],
            compiler_params=pltpu.CompilerParams(
                collective_id=0, has_side_effects=True, vmem_limit_bytes=48 << 20
            ),
            name="stitch",
        )(destinations, positions, levels, raw_tiles, flat_profile, dark_profile)

    placed = (
        P("plane", "tile", None, None, None),
        P(None, "plane", None),
        P(None, "plane", None),
        P("plane", "tile", None),
        P("plane", "tile"),
        P("plane", "tile"),
    )
    return jax.shard_map(
        per_device, mesh=mesh, in_specs=placed, out_specs=P("plane", None, "tile", None), check_vma=False
    )
```

time: 315 us -> 47.1 us (0.15)
  the two profiles are of different devices: /device:TPU:15 before, /device:TPU:2 now
where the time goes in v1:
time: 47.1 us; the launch traced here: 46.9 us
  Pallas kernels  41 us (87%)
  local copies, waits for them, and re-layouts  5.83 us (12%)
    pallas_call x1, Pallas kernels, per_device(): pl.pallas_call(functools.partial(stitch_kernel, n_tile, n_plane, width),...  41 us
    unnamed x12, local copies, waits for them, and re-layouts  5.83 us

profile of v1, /device:TPU:2, one launch (start us, length us, event | category | flops | bytes accessed | tf_op | source)
XLA Modules:
  0.0 46.9 jit_solution(2825732425948498385)
XLA Ops:
  0.0 0.7 %copy.7.dest_ref = s32[1,8,1]{2,1,0:T(8,128)S(1)} copy(s32[1,8,1]{1,2,0:T(1,128)} %param.9) | data formatting | bytes 64 | tf_op args[3]
  0.7 0.0 copy-start
  0.7 1.0 %copy-done = bf16[1,8,2,16,1024]{4,3,2,1,0:T(8,128)(2,1)S(1)} copy-done((bf16[1,8,2,16,1024]{4,3,2,1,0:T(8,128)(2,1)S(1)}, bf16[1,8,2,16,1024]{4,3,2,1,0:T(8,128)(2,1)}, u32[]{:S(2)}) %copy-start) | copy-done | bytes 524312
  1.8 0.0 copy-start.1
  1.8 0.7 %copy-done.1 = bf16[2,4,1024]{2,1,0:T(4,128)(2,1)S(1)} copy-done((bf16[2,4,1024]{2,1,0:T(4,128)(2,1)S(1)}, bf16[2,4,1024]{2,1,0:T(4,128)(2,1)}, u32[]{:S(2)}) %copy-start.1) | copy-done | bytes 16408
  2.5 0.0 copy-start.2
  2.5 0.7 %copy-done.2 = bf16[2,4,1024]{2,1,0:T(4,128)(2,1)S(1)} copy-done((bf16[2,4,1024]{2,1,0:T(4,128)(2,1)S(1)}, bf16[2,4,1024]{2,1,0:T(4,128)(2,1)}, u32[]{:S(2)}) %copy-start.2) | copy-done | bytes 16408
  3.2 0.0 copy-start.3
  3.2 0.7 %copy-done.3 = s32[1,8]{1,0:T(1,128)S(1)} copy-done((s32[1,8]{1,0:T(1,128)S(1)}, s32[1,8]{1,0:T(1,128)}, u32[]{:S(2)}) %copy-start.3) | copy-done | bytes 56
  3.9 0.0 copy-start.4
  3.9 0.7 %copy-done.4 = s32[1,8]{1,0:T(1,128)S(1)} copy-done((s32[1,8]{1,0:T(1,128)S(1)}, s32[1,8]{1,0:T(1,128)}, u32[]{:S(2)}) %copy-start.4) | copy-done | bytes 56
  4.5 41.0 %stitch.1 = bf16[1,2,512,1024]{3,2,1,0:T(8,128)(2,1)S(1)} custom-call(s32[1,8,1]{2,1,0:T(8,128)S(1)} %copy.7.dest_ref, s32[1,8]{1,0:T(1,128)S(1)} %copy-done.3, s32[1,8]{1,0:T(1,128)S(1)} %copy-done.4, bf16[1,8,2,16,1024]{4,3,2,1,0:T(8,128)(2,1)S(1)} %copy-done, bf16[2,4,1024]{2,1,0:T(4,128)(2,1)S(1)} %copy-done.1, bf16[2,4,1024]{2,1,0:T(4,128)(2,1)S(1)} %copy-done.2), custom_call_target="tpu_custom_call" | custom-call | tf_op jit(solution)/shard_map/stitch/pallas_call | solution.py:311
  45.5 1.3 %copy.9 = bf16[1,2,512,1024]{3,2,1,0:T(8,128)(2,1)} copy(bf16[1,2,512,1024]{3,2,1,0:T(8,128)(2,1)S(1)} %stitch.1) | data formatting | bytes 4194304
Async XLA Ops:
  0.7 1.0 %copy-start = (bf16[1,8,2,16,1024]{4,3,2,1,0:T(8,128)(2,1)S(1)}, bf16[1,8,2,16,1024]{4,3,2,1,0:T(8,128)(2,1)}, u32[]{:S(2)}) copy-start(bf16[1,8,2,16,1024]{4,3,2,1,0:T(8,128)(2,1)} %raw_ref.1) | copy-start | bytes 1572868
  1.8 0.7 %copy-start.1 = (bf16[2,4,1024]{2,1,0:T(4,128)(2,1)S(1)}, bf16[2,4,1024]{2,1,0:T(4,128)(2,1)}, u32[]{:S(2)}) copy-start(bf16[2,4,1024]{2,1,0:T(4,128)(2,1)} %flat_ref.1) | copy-start | bytes 49156
  2.5 0.7 %copy-start.2 = (bf16[2,4,1024]{2,1,0:T(4,128)(2,1)S(1)}, bf16[2,4,1024]{2,1,0:T(4,128)(2,1)}, u32[]{:S(2)}) copy-start(bf16[2,4,1024]{2,1,0:T(4,128)(2,1)} %dark_ref.1) | copy-start | bytes 49156
  3.2 0.7 %copy-start.3 = (s32[1,8]{1,0:T(1,128)S(1)}, s32[1,8]{1,0:T(1,128)}, u32[]{:S(2)}) copy-start(s32[1,8]{1,0:T(1,128)} %pos_ref.1) | copy-start | bytes 100
  3.9 0.7 %copy-start.4 = (s32[1,8]{1,0:T(1,128)S(1)}, s32[1,8]{1,0:T(1,128)}, u32[]{:S(2)}) copy-start(s32[1,8]{1,0:T(1,128)} %level_ref.1) | copy-start | bytes 100

commit v2 on v1

v2 whole, which is shorter than its diff:
```python
import functools

import jax
import jax.numpy as jnp
from jax import lax
from jax.experimental import pallas as pl
from jax.experimental.pallas import tpu as pltpu
from jax.sharding import PartitionSpec as P

MESH = pl.DeviceIdType.MESH
F32 = jnp.float32
BF16 = jnp.bfloat16
OWNER_ROWS = 512
TILE_ROWS = 16
NEAR = (-2, -1, 1, 2)
GROUPS = 6
DEPTH = GROUPS * 128
NEARER = 4 * 128
SPAN = 256
Q = 1.0 / 4.5
Q2 = Q * Q
Q3 = Q2 * Q


def stitch_kernel(
    n_tile, n_plane, width,
    dest_hbm, pos_hbm, level_hbm, raw_ref, flat_ref, dark_ref, out_ref,
    dest_ref, pos_ref, level_ref,
    rawv, sbuf, rbuf, smeta, rmeta, prof, dark_v, inv_v, pos_all, gain_all, g_all,
    edge, strip, sblk, rblk, sstrip, rstrip, vbuf, mbuf, acc, rim, vrim, mrim,
    raw_sem, own_sem, int_sem,
    tile_s, tile_r, meta_s, meta_r, gat_s, gat_r, side_s, side_r, swap_s, swap_r, blk_s, blk_r, str_s, str_r,
):
    me = lax.axis_index("tile")
    plane = lax.axis_index("plane")
    core = lax.rem(me, 2)
    column = lax.rem(me // 2, 4)
    up = column >= 2
    inner = jnp.logical_or(column == 1, column == 2)
    half = n_tile // 2
    reps = width // 128

    def at(offset):
        return {"tile": lax.rem(me + offset + n_tile, n_tile), "plane": plane}

    def mate(k):
        return {"tile": me, "plane": lax.rem(plane + k, n_plane)}

    barrier = pltpu.get_barrier_semaphore()
    for offset in NEAR + (half,):
        pl.semaphore_signal(barrier, inc=1, device_id=at(offset), device_id_type=MESH)

    @pl.when(inner)
    def _():
        for k in range(1, n_plane):
            pl.semaphore_signal(barrier, inc=1, device_id=mate(k), device_id_type=MESH)

    loads = [
        pltpu.make_async_copy(src, dst, int_sem.at[j])
        for j, (src, dst) in enumerate(((dest_hbm, dest_ref), (pos_hbm, pos_ref), (level_hbm, level_ref)))
    ]
    for load in loads:
        load.start()
    load_raw = pltpu.make_async_copy(raw_ref.at[0], rawv, raw_sem)
    load_raw.start()

    @pl.when(jnp.logical_and(inner, core == 0))
    def _():
        pltpu.make_async_copy(flat_ref, prof.at[0, plane], own_sem).start()

    @pl.when(jnp.logical_and(inner, core == 1))
    def _():
        pltpu.make_async_copy(dark_ref, prof.at[1, plane], own_sem).start()

    for load in loads:
        load.wait()
    rel = [lax.rem(dest_ref[0, t] - me + 2 + 2 * n_tile, n_tile) for t in range(8)]
    picks = []
    for e, offset in enumerate(NEAR + (half, 0)):
        key = offset + 2
        first, last, hits = jnp.int32(0), jnp.int32(0), jnp.int32(0)
        for t in range(8):
            hit = rel[t] == key
            last = jnp.where(hit, t, last)
            hits = hits + jnp.where(hit, 1, 0)
            first = jnp.where(rel[7 - t] == key, 7 - t, first)
        gain0 = jnp.where(hits > 0, level_ref[0, first], 0).astype(F32)
        gain1 = jnp.where(hits > 1, level_ref[0, last], 0).astype(F32)
        pos0 = pos_ref[0, first].astype(F32)
        pos1 = pos_ref[0, last].astype(F32)
        row = lax.broadcasted_iota(jnp.int32, (8, 128), 0)
        meta = jnp.where(row == 0, pos0, jnp.where(row == 1, pos1, jnp.where(row == 2, gain0, gain1)))
        smeta[e] = meta
        if e == 5:
            rmeta[5] = meta
        picks.append((first, last))
    load_raw.wait()
    for e, (first, last) in enumerate(picks):
        if e == 5:
            rbuf[5, 0] = rawv[first]
            rbuf[5, 1] = rawv[last]
        else:
            sbuf[e, 0] = rawv[first]
            sbuf[e, 1] = rawv[last]

    @pl.when(inner)
    def _():
        pltpu.make_async_copy(flat_ref, prof.at[core, plane], own_sem).wait()
        pl.semaphore_wait(barrier, 4 + n_plane)

    @pl.when(jnp.logical_not(inner))
    def _():
        pl.semaphore_wait(barrier, 5)

    sends = []

    def remote(src, dst, s_sem, r_sem, device):
        return pltpu.make_async_remote_copy(src, dst, s_sem, r_sem, device_id=device, device_id_type=MESH)

    def send(src, dst, s_sem, r_sem, device):
        copy = remote(src, dst, s_sem, r_sem, device)
        copy.start()
        sends.append(copy)

    def slot_at_target(e):
        return 3 - e if e < 4 else 4

    for e, offset in enumerate(NEAR + (half,)):
        f = slot_at_target(e)
        send(smeta.at[e], rmeta.at[f], meta_s.at[e], meta_r.at[f], at(offset))

    @pl.when(inner)
    def _():
        for k in range(1, n_plane):
            remote(prof.at[core, plane], prof.at[core, plane], gat_s.at[k], gat_r.at[plane], mate(k)).start()

    for j in range(2):
        e = jnp.where(up, 3 - j, j)
        offset = jnp.where(up, 2 - j, j - 2)
        for k in range(2):
            send(sbuf.at[e, k], rbuf.at[3 - e, k], tile_s.at[e, k], tile_r.at[3 - e, k], at(offset))
    for k in range(2):
        send(sbuf.at[4, k], rbuf.at[4, k], tile_s.at[4, k], tile_r.at[4, k], at(half))
    for j in range(2):
        e = jnp.where(up, j, 3 - j)
        offset = jnp.where(up, j - 2, 2 - j)
        for k in range(2):
            send(sbuf.at[e, k], rbuf.at[3 - e, k], tile_s.at[e, k], tile_r.at[3 - e, k], at(offset))

    beside = at(jnp.where(up, 2, -2))
    to_side = remote(prof.at[core], prof.at[core], side_s, side_r, beside)

    @pl.when(inner)
    def _():
        for k in range(1, n_plane):
            source = lax.rem(plane + k, n_plane)
            remote(prof.at[core, source], prof.at[core, source], gat_s.at[k], gat_r.at[source], mate(k)).wait_recv()
        to_side.start()

    @pl.when(jnp.logical_not(inner))
    def _():
        to_side.wait_recv()

    other = {"tile": me + 1 - 2 * core, "plane": plane}
    send(prof.at[core], prof.at[core], swap_s, swap_r, other)

    row16 = lax.broadcasted_iota(jnp.int32, (TILE_ROWS, 128), 0)
    ramp = jnp.minimum(row16 + 1, TILE_ROWS - row16).astype(F32)
    lane = lax.broadcasted_iota(jnp.int32, (1, 128), 1)
    gap = lax.rem(lane // TILE_ROWS, 4).astype(F32)
    lane_row = lax.rem(lane, TILE_ROWS).astype(F32)
    lane16 = lax.broadcasted_iota(jnp.int32, (TILE_ROWS, 128), 1)
    is_first, is_last = lane16 == 0, lane16 == 127

    def wide(x):
        return jnp.concatenate([x] * reps, axis=1)

    y32 = lax.broadcasted_iota(jnp.int32, (32, 128), 0)
    y32 = jnp.where(y32 < 16, y32, y32 + OWNER_ROWS - 32).astype(F32)
    rim_row = jnp.where(lane_row < 8, lane_row + OWNER_ROWS, lane_row - 16.0)
    mrim[...] = jnp.where(jnp.abs(y32 - rim_row) == gap, 1.0, 0.0).astype(BF16)[:, 0:64]
    edge[...] = jnp.zeros(edge.shape, F32)
    pos_all[...] = jnp.full((16, 128), -99.0, F32)
    gain_all[...] = jnp.zeros((16, 128), F32)

    remote(prof.at[1 - core], prof.at[1 - core], swap_s, swap_r, other).wait_recv()
    part = TILE_ROWS // n_plane
    for p in range(n_plane):
        inv_v[:, p * part:(p + 1) * part, :] = 1.0 / prof[0, p].astype(F32)
        dark_v[:, p * part:(p + 1) * part, :] = prof[1, p].astype(F32)

    for e in range(4):
        lo, at_pos = (8, 31.0) if e < 2 else (0, 0.0)
        for ch in range(2):
            total = None
            for k in range(2):
                keep = jnp.where(smeta[e, k:k + 1, :] == at_pos, 1.0, 0.0)
                scale = wide(ramp[lo:lo + 8] * smeta[e, 2 + k:3 + k, :])
                tile = sbuf[e, k, ch].astype(F32)[lo:lo + 8]
                w = (tile - dark_v[ch, lo:lo + 8]) * inv_v[ch, lo:lo + 8] * scale
                w = w.astype(BF16).astype(F32) * wide(jnp.broadcast_to(keep, (8, 128)))
                total = w if total is None else total + w
            strip[e, ch] = total
    for j, (e, offset) in enumerate(((0, -1), (3, 1))):
        sstrip[j] = jnp.concatenate([strip[e, 0], strip[e, 1]], axis=0).astype(BF16)
        send(sstrip.at[j], rstrip.at[1 - j], str_s.at[j], str_r.at[1 - j], at(offset))

    order = (5, 4) + tuple(jnp.where(up, a, 3 - a) for a in (1, 0, 2, 3))
    for f in range(5):
        remote(smeta.at[f], rmeta.at[f], meta_s.at[f], meta_r.at[f], at(1)).wait_recv()
    for m in range(6):
        pos_all[2 * m:2 * m + 2] = rmeta[order[m], 0:2]
        gain_all[2 * m:2 * m + 2] = rmeta[order[m], 2:4]
    positions, gains = pos_all[...], gain_all[...]

    def gain_sum(p):
        return jnp.sum(jnp.where(positions == p, gains, 0.0), axis=0, keepdims=True)

    for j in range(12):
        g_all[j:j + 1] = gain_sum(positions[j:j + 1])
    gain_first, gain_last = gain_sum(0.0), gain_sum(31.0)

    y = lax.broadcasted_iota(jnp.int32, (OWNER_ROWS, 128), 0).astype(F32)
    y16 = lax.broadcasted_iota(jnp.int32, (16, 128), 0).astype(F32)
    top_shift = jnp.where(me == 0, 2.0, 1e6).astype(F32)
    bottom_shift = jnp.where(me == n_tile - 1, -1.0 * OWNER_ROWS - 16.0, 1e6).astype(F32)

    def place(m):
        p0, p1 = pos_all[2 * m:2 * m + 1], pos_all[2 * m + 1:2 * m + 2]
        source_row = jnp.where(lane < 64, p0, p1) * TILE_ROWS + lane_row
        cols = slice(m * 128, (m + 1) * 128)

        def hits(d):
            return jnp.where(jnp.abs(d) == gap, 1.0, 0.0)

        mbuf[:, cols] = hits(y - source_row).astype(BF16)
        mbuf[0:16, cols] = (hits(y16 - source_row) - hits(y16 + source_row + top_shift)).astype(BF16)
        low = OWNER_ROWS - 16.0
        mbuf[OWNER_ROWS - 16:, cols] = (
            hits(y16 + low - source_row) - hits(y16 + source_row + bottom_shift)
        ).astype(BF16)

    def sides(pieces, ends):
        right = [pltpu.roll(x, 1, 1) for x in pieces]
        left = [pltpu.roll(x, 127, 1) for x in pieces]
        zero = jnp.zeros_like(pieces[0])
        before = [zero if ends[0] else right[0]] + right[:-1]
        after = left[1:] + [zero if ends[1] else left[-1]]
        return [
            jnp.where(is_first, a, b) + jnp.where(is_last, d, c)
            for a, b, c, d in zip(before, right, left, after)
        ]

    def spread(b_of, put):
        middle = reps // 2
        for lo, hi, keep in ((0, middle + 1, (0, middle)), (middle - 1, reps, (1, middle + 1))):
            b = [b_of(i) for i in range(lo, hi)]
            ends = (lo == 0, hi == reps)
            kept = slice(*keep)
            two = [(0.5 * Q3) * x for x in b[kept]]
            zero = [(0.5 * Q) * x for x in b[kept]]
            one = [(0.5 * Q2 + 3.0 * Q3) * x for x in b[kept]]
            three = [Q3 * x for x in b[kept]]
            c = sides(b, ends)
            two = [t + (3.0 * Q3) * x for t, x in zip(two, c[kept])]
            zero = [t + (0.5 * Q2) * x for t, x in zip(zero, c[kept])]
            one = [t + Q3 * x for t, x in zip(one, c[kept])]
            c = sides(c, ends)
            zero = [t + (0.5 * Q3) * x + 2.0 * s for t, x, s in zip(zero, c[kept], two)]
            one = [t + (3.0 * Q3) * x for t, x in zip(one, c[kept])]
            c = sides(c, ends)
            zero = [t + Q3 * x for t, x in zip(zero, c[kept])]
            first = (lo + keep[0]) * 128
            for d, v in enumerate((zero, one, two, three)):
                put(d, first, jnp.concatenate(v, axis=1).astype(BF16))

    last_row = jnp.where(up, 31.0, 0.0).astype(F32)
    other_row = jnp.where(up, 0.0, 31.0).astype(F32)

    def work(m):
        e = order[m]
        for k in range(2):
            if m > 0:
                remote(sbuf.at[0, k], rbuf.at[e, k], tile_s.at[0, k], tile_r.at[e, k], at(1)).wait_recv()
            j = 2 * m + k
            p = pos_all[j:j + 1]
            keep_near = jnp.broadcast_to(jnp.where(p == last_row, 1.0, 0.0), (8, 128))
            keep_far = jnp.broadcast_to(jnp.where(p == other_row, 1.0, 0.0), (8, 128))
            scale = ramp * gain_all[j:j + 1]
            share = 1.0 / jnp.maximum(ramp * g_all[j:j + 1], 1.0)

            def unit(ch, carry):
                def weighted(i):
                    lanes = slice(i * 128, i * 128 + 128)
                    w = (rbuf[e, k, ch, :, lanes].astype(F32) - dark_v[ch, :, lanes]) * inv_v[ch, :, lanes] * scale
                    return w.astype(BF16).astype(F32)

                def scaled(i):
                    return weighted(i) * share

                for i in range(reps):
                    w = weighted(i)
                    lanes = slice(i * 128, i * 128 + 128)
                    if m < 4:
                        edge[0, ch, :, lanes] += keep_near * jnp.where(up, w[8:16], w[0:8])
                    if m < 2 or m >= 4:
                        edge[1, ch, :, lanes] += keep_far * jnp.where(up, w[0:8], w[8:16])

                def put(d, first, v):
                    start = m * 128 + k * 64 + d * TILE_ROWS
                    vbuf[ch, start:start + TILE_ROWS, first:first + v.shape[1]] = v

                spread(scaled, put)
                return carry

            lax.fori_loop(0, 2, unit, 0)

    def send_edge(j):
        down = up if j == 0 else jnp.logical_not(up)
        total = jnp.where(down, gain_last, gain_first)
        mark = lax.broadcasted_iota(jnp.int32, (8, width), 0) == 4
        block = [jnp.where(mark, wide(jnp.broadcast_to(total, (8, 128))), edge[j, ch]) for ch in range(2)]
        sblk[j] = jnp.concatenate(block, axis=0).astype(BF16)
        offset = jnp.where(down, 1, -1)
        lands = jnp.where(down, 0, 1)
        send(sblk.at[j], rblk.at[lands], blk_s.at[j], blk_r.at[lands], at(offset))

    for m in range(4):
        work(m)
    send_edge(0)
    for m in range(GROUPS):
        place(m)

    per_channel = width // SPAN

    def chunk(n):
        return n // per_channel, pl.ds(pl.multiple_of(lax.rem(n, per_channel) * SPAN, SPAN), SPAN)

    def nearer(n, carry):
        ch, cols = chunk(n)
        acc[ch, :, cols] = jnp.dot(
            mbuf[:, 0:NEARER], vbuf[ch, 0:NEARER, cols], preferred_element_type=F32
        )
        return carry

    lax.fori_loop(0, 2 * per_channel, nearer, 0)

    for m in range(4, GROUPS):
        work(m)
    send_edge(1)

    def farther(n, carry):
        ch, cols = chunk(n)
        made = acc[ch, :, cols] + jnp.dot(
            mbuf[:, NEARER:], vbuf[ch, NEARER:, cols], preferred_element_type=F32
        )
        out_ref[0, ch, :, cols] = made.astype(BF16)
        rim[ch, 0:16, cols] = made[0:16]
        rim[ch, 16:32, cols] = made[OWNER_ROWS - 16:]
        return carry

    lax.fori_loop(0, 2 * per_channel, farther, 0)

    for j in range(2):
        remote(sstrip.at[j], rstrip.at[j], str_s.at[j], str_r.at[j], at(1)).wait_recv()
        remote(sblk.at[j], rblk.at[j], blk_s.at[j], blk_r.at[j], at(1)).wait_recv()
    shares = []
    for j in range(2):
        inside = jnp.where(me == (0 if j == 0 else n_tile - 1), 0.0, 1.0).astype(F32)
        lo = 8 - 8 * j
        total = rblk[j].astype(F32)[4:5, 0:128]
        shares.append(inside / jnp.maximum(total * ramp[lo:lo + 8], 1.0))

    def beside_rows(ch, carry):
        start = pl.multiple_of(8 * ch, 8)

        def rows(i):
            lanes = slice(i * 128, i * 128 + 128)
            made = []
            for j in range(2):
                got = jnp.where(ch == 0, rblk[j, :, lanes].astype(F32)[0:8], rblk[j, :, lanes].astype(F32)[8:16])
                direct = jnp.where(
                    ch == 0, rstrip[1 - j, :, lanes].astype(F32)[0:8], rstrip[1 - j, :, lanes].astype(F32)[8:16]
                )
                made.append((got + direct + strip[1 + j, ch, :, lanes]) * shares[j])
            return jnp.concatenate([made[1], made[0]], axis=0)

        def put(d, first, v):
            vrim[ch, d * TILE_ROWS:(d + 1) * TILE_ROWS, first:first + v.shape[1]] = v

        spread(rows, put)
        for first in range(0, width, SPAN):
            cols = slice(first, first + SPAN)
            made = rim[ch, :, cols] + jnp.dot(mrim[...], vrim[ch, :, cols], preferred_element_type=F32)
            out_ref[0, ch, 0:16, cols] = made[0:16].astype(BF16)
            out_ref[0, ch, OWNER_ROWS - 16:, cols] = made[16:32].astype(BF16)
        return carry

    lax.fori_loop(0, 2, beside_rows, 0)

    for copy in sends:
        copy.wait_send()

    @pl.when(inner)
    def _():
        for k in range(1, n_plane):
            remote(prof.at[core, plane], prof.at[core, plane], gat_s.at[k], gat_r.at[plane], mate(k)).wait_send()
        to_side.wait_send()


def solution(mesh):
    n_tile, n_plane = mesh.shape["tile"], mesh.shape["plane"]

    def per_device(raw_tiles, flat_profile, dark_profile, destinations, positions, levels):
        width = raw_tiles.shape[-1]
        tile = (2, TILE_ROWS, width)
        dma = pltpu.SemaphoreType.DMA
        return pl.pallas_call(
            functools.partial(stitch_kernel, n_tile, n_plane, width),
            out_shape=pltpu.VMEM((1, 2, OWNER_ROWS, width), BF16),
            in_specs=[pl.BlockSpec(memory_space=pltpu.HBM)] * 6,
            out_specs=pl.BlockSpec(memory_space=pltpu.VMEM),
            scratch_shapes=[
                pltpu.SMEM((1, 8), jnp.int32),
                pltpu.SMEM((1, 8), jnp.int32),
                pltpu.SMEM((1, 8), jnp.int32),
                pltpu.VMEM((8,) + tile, BF16),
                pltpu.VMEM((5, 2) + tile, BF16),
                pltpu.VMEM((6, 2) + tile, BF16),
                pltpu.VMEM((6, 8, 128), F32),
                pltpu.VMEM((6, 8, 128), F32),
                pltpu.VMEM((2, n_plane, 2, TILE_ROWS // n_plane, width), BF16),
                pltpu.VMEM(tile, F32),
                pltpu.VMEM(tile, F32),
                pltpu.VMEM((16, 128), F32),
                pltpu.VMEM((16, 128), F32),
                pltpu.VMEM((16, 128), F32),
                pltpu.VMEM((2, 2, 8, width), F32),
                pltpu.VMEM((4, 2, 8, width), F32),
                pltpu.VMEM((2, 16, width), BF16),
                pltpu.VMEM((2, 16, width), BF16),
                pltpu.VMEM((2, 16, width), BF16),
                pltpu.VMEM((2, 16, width), BF16),
                pltpu.VMEM((2, DEPTH, width), BF16),
                pltpu.VMEM((OWNER_ROWS, DEPTH), BF16),
                pltpu.VMEM((2, OWNER_ROWS, width), F32),
                pltpu.VMEM((2, 32, width), F32),
                pltpu.VMEM((2, 64, width), BF16),
                pltpu.VMEM((32, 64), BF16),
                dma, dma, dma((3,)),
                dma((5, 2)), dma((5, 2)), dma((5,)), dma((5,)),
                dma((n_plane,)), dma((n_plane,)), dma, dma, dma, dma,
                dma((2,)), dma((2,)), dma((2,)), dma((2,)),
            ],
            compiler_params=pltpu.CompilerParams(
                collective_id=0, has_side_effects=True, vmem_limit_bytes=(62 << 20) - (64 << 10)
            ),
            name="stitch",
        )(destinations[:, :, 0], positions, levels, raw_tiles, flat_profile, dark_profile)

    placed = (
        P("plane", "tile", None, None, None),
        P(None, "plane", None),
        P(None, "plane", None),
        P("plane", "tile", None),
        P("plane", "tile"),
        P("plane", "tile"),
    )
    return jax.shard_map(
        per_device, mesh=mesh, in_specs=placed, out_specs=P("plane", None, "tile", None), check_vma=False
    )
```

time: 47.1 us -> 34.6 us (0.73)
  the two profiles are of different devices: /device:TPU:2 before, /device:TPU:32 now
where the time goes in v2:
time: 34.6 us; the launch traced here: 34.5 us
  Pallas kernels  33.2 us (96%)
  local copies, waits for them, and re-layouts  1.32 us (4%)
    pallas_call x1, Pallas kernels, per_device(): pl.pallas_call(functools.partial(stitch_kernel, n_tile, n_plane, width),...  33.2 us
    unnamed x1, local copies, waits for them, and re-layouts  1.32 us

profile of v2, /device:TPU:32, one launch (start us, length us, event | category | flops | bytes accessed | tf_op | source)
XLA Modules:
  0.0 34.5 jit_solution(12995461075180465749)
XLA Ops:
  0.0 33.2 %stitch.1 = bf16[1,2,512,1024]{3,2,1,0:T(8,128)(2,1)S(1)} custom-call(s32[1,8]{1,0:T(1,128)} %bitcast.1, s32[1,8]{1,0:T(1,128)} %pos_hbm.1, s32[1,8]{1,0:T(1,128)} %level_hbm.1, bf16[1,8,2,16,1024]{4,3,2,1,0:T(8,128)(2,1)} %raw_ref.1, bf16[2,4,1024]{2,1,0:T(4,128)(2,1)} %flat_ref.1, bf16[2,4,1024]{2,1,0:T(4,128)(2,1)} %dark_ref.1), custom_call_target="tpu_custom_call" | custom-call | tf_op jit(solution)/shard_map/stitch/pallas_call | solution.py:418
  33.2 1.3 %copy.8 = bf16[1,2,512,1024]{3,2,1,0:T(8,128)(2,1)} copy(bf16[1,2,512,1024]{3,2,1,0:T(8,128)(2,1)S(1)} %stitch.1) | data formatting | bytes 4194304

commit v3 on v2

v3 whole, which is shorter than its diff:
```python
import functools

import jax
import jax.numpy as jnp
from jax import lax
from jax.experimental import pallas as pl
from jax.experimental.pallas import tpu as pltpu
from jax.sharding import PartitionSpec as P

MESH = pl.DeviceIdType.MESH
F32 = jnp.float32
BF16 = jnp.bfloat16
OWNER_ROWS = 512
TILE_ROWS = 16
NEAR = (-2, -1, 1, 2)
GROUPS = 6
DEPTH = GROUPS * 128
NEARER = 4 * 128
SPAN = 1024
Q = 1.0 / 4.5
Q2 = Q * Q
Q3 = Q2 * Q


def stitch_kernel(
    n_tile, n_plane, width,
    dest_hbm, pos_hbm, level_hbm, raw_ref, flat_ref, dark_ref, out_ref,
    dest_ref, pos_ref, level_ref,
    rawv, sbuf, rbuf, smeta, rmeta, prof, dark_v, inv_v, pos_all, gain_all, g_all,
    edge, strip, sblk, rblk, passing, wbuf, vbuf, mbuf, acc, rim, vrim, mrim,
    raw_sem, own_sem, int_sem, go_sem,
    tile_s, tile_r, meta_s, meta_r, gat_s, gat_r, side_s, side_r, swap_s, swap_r, blk_s, blk_r, pass_s, pass_r,
):
    me = lax.axis_index("tile")
    plane = lax.axis_index("plane")
    core = lax.rem(me, 2)
    column = lax.rem(me // 2, 4)
    up = column >= 2
    inner = jnp.logical_or(column == 1, column == 2)
    half = n_tile // 2
    reps = width // 128

    def at(offset):
        return {"tile": lax.rem(me + offset + n_tile, n_tile), "plane": plane}

    def mate(k):
        return {"tile": me, "plane": lax.rem(plane + k, n_plane)}

    def late_of(device):
        return lax.rem(device // 8, 2)

    is_late = late_of(me)
    late = is_late == 1
    early = is_late == 0
    outer = jnp.logical_not(inner)
    far = jnp.where(up, 3, 0)
    far_offset = jnp.where(up, 2, -2)
    next_far = jnp.where(up, 2, 1)
    next_crosses = core == jnp.where(up, 1, 0)
    crossing = jnp.where(next_crosses, 2, 1)

    def crosses(offset):
        return late_of(lax.rem(me + offset + n_tile, n_tile)) != is_late

    barrier = pltpu.get_barrier_semaphore()
    for offset in NEAR + (half,):
        @pl.when(jnp.logical_or(early, jnp.logical_not(crosses(offset))))
        def _():
            pl.semaphore_signal(barrier, inc=1, device_id=at(offset), device_id_type=MESH)

    @pl.when(inner)
    def _():
        for k in range(1, n_plane):
            pl.semaphore_signal(barrier, inc=1, device_id=mate(k), device_id_type=MESH)

    @pl.when(early)
    def _():
        pl.semaphore_signal(barrier, inc=1, device_id=at(2 * far_offset), device_id_type=MESH)

    loads = [
        pltpu.make_async_copy(src, dst, int_sem.at[j])
        for j, (src, dst) in enumerate(((dest_hbm, dest_ref), (pos_hbm, pos_ref), (level_hbm, level_ref)))
    ]
    for load in loads:
        load.start()
    load_raw = pltpu.make_async_copy(raw_ref.at[0], rawv, raw_sem)
    load_raw.start()

    @pl.when(jnp.logical_and(inner, core == 0))
    def _():
        pltpu.make_async_copy(flat_ref, prof.at[0, plane], own_sem).start()

    @pl.when(jnp.logical_and(inner, core == 1))
    def _():
        pltpu.make_async_copy(dark_ref, prof.at[1, plane], own_sem).start()

    for load in loads:
        load.wait()
    rel = [lax.rem(dest_ref[0, t] - me + 2 + 2 * n_tile, n_tile) for t in range(8)]
    picks = []
    for e, offset in enumerate(NEAR + (half, 0)):
        key = offset + 2
        first, last, hits = jnp.int32(0), jnp.int32(0), jnp.int32(0)
        for t in range(8):
            hit = rel[t] == key
            last = jnp.where(hit, t, last)
            hits = hits + jnp.where(hit, 1, 0)
            first = jnp.where(rel[7 - t] == key, 7 - t, first)
        gain0 = jnp.where(hits > 0, level_ref[0, first], 0).astype(F32)
        gain1 = jnp.where(hits > 1, level_ref[0, last], 0).astype(F32)
        pos0 = pos_ref[0, first].astype(F32)
        pos1 = pos_ref[0, last].astype(F32)
        row = lax.broadcasted_iota(jnp.int32, (8, 128), 0)
        meta = jnp.where(row == 0, pos0, jnp.where(row == 1, pos1, jnp.where(row == 2, gain0, gain1)))
        smeta[e] = meta
        if e == 5:
            rmeta[5] = meta
        picks.append((first, last))
    load_raw.wait()
    for e, (first, last) in enumerate(picks):
        if e == 5:
            rbuf[5, 0] = rawv[first]
            rbuf[5, 1] = rawv[last]
        else:
            sbuf[e, 0] = rawv[first]
            sbuf[e, 1] = rawv[last]

    @pl.when(inner)
    def _():
        pltpu.make_async_copy(flat_ref, prof.at[core, plane], own_sem).wait()

    pl.semaphore_wait(barrier, jnp.where(inner, 4 + n_plane + is_late, jnp.where(late, 6, 5 - crossing)))

    @pl.when(late)
    def _():
        for offset in NEAR:
            @pl.when(crosses(offset))
            def _():
                pl.semaphore_signal(go_sem, inc=1, device_id=at(offset), device_id_type=MESH)

    @pl.when(jnp.logical_and(late, outer))
    def _():
        pl.semaphore_signal(go_sem, inc=1, device_id=at(2 * far_offset), device_id_type=MESH)

    sends = []

    def remote(src, dst, s_sem, r_sem, device):
        return pltpu.make_async_remote_copy(src, dst, s_sem, r_sem, device_id=device, device_id_type=MESH)

    def send(src, dst, s_sem, r_sem, device):
        copy = remote(src, dst, s_sem, r_sem, device)
        copy.start()
        sends.append(copy)

    def slot_at_target(e):
        return 3 - e if e < 4 else 4

    def send_meta(e):
        f = slot_at_target(e)
        return remote(smeta.at[e], rmeta.at[f], meta_s.at[e], meta_r.at[f], at((NEAR + (half,))[e]))

    for e, offset in enumerate(NEAR + (half,)):
        @pl.when(jnp.logical_or(late, jnp.logical_not(crosses(offset))))
        def _():
            send_meta(e).start()

    @pl.when(inner)
    def _():
        for k in range(1, n_plane):
            remote(prof.at[core, plane], prof.at[core, plane], gat_s.at[k], gat_r.at[plane], mate(k)).start()

    def send_tile(e, k, offset):
        return remote(sbuf.at[e, k], rbuf.at[3 - e, k], tile_s.at[e, k], tile_r.at[3 - e, k], at(offset))

    def send_far():
        send_tile(far, 0, far_offset).start()

    def send_next():
        for k in range(2):
            send_tile(next_far, k, jnp.where(up, 1, -1)).start()

    def send_near():
        for j in range(2):
            e = jnp.where(up, j, 3 - j)
            for k in range(2):
                send_tile(e, k, jnp.where(up, j - 2, 2 - j)).start()

    @pl.when(jnp.logical_not(inner))
    def _():
        remote(sbuf.at[far, 1], passing, tile_s.at[far, 1], pass_r, at(-far_offset)).start()

    @pl.when(jnp.logical_and(outer, late))
    def _():
        send_far()

    @pl.when(jnp.logical_and(outer, jnp.logical_or(late, jnp.logical_not(next_crosses))))
    def _():
        send_next()

    for k in range(2):
        send(sbuf.at[4, k], rbuf.at[4, k], tile_s.at[4, k], tile_r.at[4, k], at(half))

    @pl.when(jnp.logical_not(inner))
    def _():
        send_near()

    to_side = remote(prof.at[core], prof.at[core], side_s, side_r, at(far_offset))
    pass_on = remote(passing, rbuf.at[3 - far, 1], pass_s, tile_r.at[3 - far, 1], at(2 * far_offset))
    def forward():
        remote(sbuf.at[far, 1], passing, tile_s.at[far, 1], pass_r, at(-far_offset)).wait_recv()
        pass_on.start()

    @pl.when(jnp.logical_and(inner, late))
    def _():
        forward()

    @pl.when(inner)
    def _():
        for k in range(1, n_plane):
            source = lax.rem(plane + k, n_plane)
            remote(prof.at[core, source], prof.at[core, source], gat_s.at[k], gat_r.at[source], mate(k)).wait_recv()
        to_side.start()
        send_tile(far, 1, far_offset).start()
        send_far()
        send_next()
        send_near()

    @pl.when(jnp.logical_not(inner))
    def _():
        to_side.wait_recv()

    other = {"tile": me + 1 - 2 * core, "plane": plane}
    send(prof.at[core], prof.at[core], swap_s, swap_r, other)

    row16 = lax.broadcasted_iota(jnp.int32, (TILE_ROWS, 128), 0)
    ramp = jnp.minimum(row16 + 1, TILE_ROWS - row16).astype(F32)
    lane = lax.broadcasted_iota(jnp.int32, (1, 128), 1)
    gap = lax.rem(lane // TILE_ROWS, 4).astype(F32)
    lane_row = lax.rem(lane, TILE_ROWS).astype(F32)
    lane16 = lax.broadcasted_iota(jnp.int32, (TILE_ROWS, 128), 1)
    lane_b = lane16.astype(F32).astype(BF16)

    def wide(x):
        return jnp.concatenate([x] * reps, axis=1)

    y32 = lax.broadcasted_iota(jnp.int32, (32, 128), 0)
    y32 = jnp.where(y32 < 16, y32, y32 + OWNER_ROWS - 32).astype(F32)
    rim_row = lax.rem(lane, 8).astype(F32)
    rim_row = jnp.where(rim_row < 4, rim_row + OWNER_ROWS, rim_row - 8.0)
    rim_hit = jnp.where(jnp.abs(y32 - rim_row) == gap, 1.0, 0.0)
    for ch in range(2):
        own = lax.rem(lane // 8, 2) == ch
        mrim[ch] = jnp.where(own, rim_hit, 0.0).astype(BF16)[:, 0:64]
    edge[...] = jnp.zeros(edge.shape, F32)
    pos_all[...] = jnp.full((16, 128), -99.0, F32)
    gain_all[...] = jnp.zeros((16, 128), F32)

    remote(prof.at[1 - core], prof.at[1 - core], swap_s, swap_r, other).wait_recv()
    part = TILE_ROWS // n_plane
    for p in range(n_plane):
        inv_v[:, p * part:(p + 1) * part, :] = 1.0 / prof[0, p].astype(F32)
        dark_v[:, p * part:(p + 1) * part, :] = prof[1, p].astype(F32)

    row_wide = lax.broadcasted_iota(jnp.int32, (TILE_ROWS, width), 0)
    gain_row = jnp.logical_or(row_wide == 3, row_wide == 12)
    gain_row16 = jnp.logical_or(row16 == 3, row16 == 12)

    for e in range(4):
        lo, at_pos = (8, 31.0) if e < 2 else (0, 0.0)
        for ch in range(2):
            total = None
            for k in range(2):
                keep = jnp.where(smeta[e, k:k + 1, :] == at_pos, 1.0, 0.0)
                scale = wide(ramp[lo:lo + 8] * smeta[e, 2 + k:3 + k, :])
                tile = sbuf[e, k, ch].astype(F32)[lo:lo + 8]
                w = (tile - dark_v[ch, lo:lo + 8]) * inv_v[ch, lo:lo + 8] * scale
                w = jnp.where(gain_row[lo:lo + 8], wide(smeta[e, 2 + k:3 + k, :]), w.astype(BF16).astype(F32))
                w = w * wide(jnp.broadcast_to(keep, (8, 128)))
                total = w if total is None else total + w
            strip[e, ch] = total
    order = (5, 4) + tuple(jnp.where(up, a, 3 - a) for a in (1, 0, 2, 3))

    def take_meta(m):
        if m > 0:
            f = order[m]
            remote(smeta.at[0], rmeta.at[f], meta_s.at[0], meta_r.at[f], at(1)).wait_recv()
        pos_all[2 * m:2 * m + 2] = rmeta[order[m], 0:2]
        gain_all[2 * m:2 * m + 2] = rmeta[order[m], 2:4]

    for m in range(4):
        take_meta(m)

    y = lax.broadcasted_iota(jnp.int32, (OWNER_ROWS, 128), 0).astype(F32)
    y16 = lax.broadcasted_iota(jnp.int32, (16, 128), 0).astype(F32)
    top_shift = jnp.where(me == 0, 2.0, 1e6).astype(F32)
    bottom_shift = jnp.where(me == n_tile - 1, -1.0 * OWNER_ROWS - 16.0, 1e6).astype(F32)

    def place(m):
        p0, p1 = pos_all[2 * m:2 * m + 1], pos_all[2 * m + 1:2 * m + 2]
        source_row = jnp.where(lane < 64, p0, p1) * TILE_ROWS + lane_row
        cols = slice(m * 128, (m + 1) * 128)

        def hits(d):
            return jnp.where(jnp.abs(d) == gap, 1.0, 0.0)

        mbuf[:, cols] = hits(y - source_row).astype(BF16)
        mbuf[0:16, cols] = (hits(y16 - source_row) - hits(y16 + source_row + top_shift)).astype(BF16)
        low = OWNER_ROWS - 16.0
        mbuf[OWNER_ROWS - 16:, cols] = (
            hits(y16 + low - source_row) - hits(y16 + source_row + bottom_shift)
        ).astype(BF16)

    def spread(pieces, share, put):
        nothing = jnp.zeros((TILE_ROWS, 128), BF16)
        right, left = {}, {}
        for d in (1, 2, 3):
            right[d] = [pltpu.roll(x, d, 1) for x in pieces]
            left[d] = [pltpu.roll(x, 128 - d, 1) for x in pieces]
        for i in range(reps):
            x = pieces[i].astype(F32)
            s = {}
            for d in (1, 2, 3):
                r = jnp.where(lane_b < d, right[d][i - 1] if i else nothing, right[d][i]).astype(F32)
                l = jnp.where(lane_b >= 128 - d, left[d][i + 1] if i + 1 < reps else nothing, left[d][i]).astype(F32)
                s[d] = r + l
                if d == 1:
                    r1, l1 = r, l
            second, third = s[2], s[3]
            if i == 0:
                second = second - jnp.where(lane16 == 0, x, 0.0)
                third = third - jnp.where(lane16 == 0, l1, jnp.where(lane16 == 1, r1, 0.0))
            if i == reps - 1:
                second = second - jnp.where(lane16 == 127, x, 0.0)
                third = third - jnp.where(lane16 == 127, r1, jnp.where(lane16 == 126, l1, 0.0))
            zero = (0.5 * Q + 2.0 * Q3) * x + (0.5 * Q2 + 9.0 * Q3) * s[1] + (0.5 * Q3) * second + Q3 * third
            one = (0.5 * Q2 + 9.0 * Q3) * x + Q3 * s[1] + (3.0 * Q3) * second
            two = (0.5 * Q3) * x + (3.0 * Q3) * s[1]
            for d, v in enumerate((zero, one, two, Q3 * x)):
                put(d, slice(i * 128, i * 128 + 128), (v * share).astype(BF16))

    last_row = jnp.where(up, 31.0, 0.0).astype(F32)
    other_row = jnp.where(up, 0.0, 31.0).astype(F32)

    def weigh(m, k):
        e = order[m]
        if m > 0:
            remote(sbuf.at[0, k], rbuf.at[e, k], tile_s.at[0, k], tile_r.at[e, k], at(1)).wait_recv()
        j = 2 * m + k
        p = pos_all[j:j + 1]
        keep_near = jnp.broadcast_to(jnp.where(p == last_row, 1.0, 0.0), (8, 128))
        keep_far = jnp.broadcast_to(jnp.where(p == other_row, 1.0, 0.0), (8, 128))
        scale = ramp * gain_all[j:j + 1]

        def unit(ch, carry):
            for i in range(reps):
                lanes = slice(i * 128, i * 128 + 128)
                w = (rbuf[e, k, ch, :, lanes].astype(F32) - dark_v[ch, :, lanes]) * inv_v[ch, :, lanes] * scale
                w = w.astype(BF16)
                wbuf[j, ch, :, lanes] = w
                w = jnp.where(gain_row16, gain_all[j:j + 1], w.astype(F32))
                if m < 4:
                    edge[0, ch, :, lanes] += keep_near * jnp.where(up, w[8:16], w[0:8])
                if m < 2 or m >= 4:
                    edge[1, ch, :, lanes] += keep_far * jnp.where(up, w[0:8], w[8:16])
            return carry

        lax.fori_loop(0, 2, unit, 0)

    def filter_columns(m, k):
        j = 2 * m + k
        share = 1.0 / jnp.maximum(ramp * g_all[j:j + 1], 1.0)

        def unit(ch, carry):
            def put(d, lanes, v):
                start = m * 128 + k * 64 + d * TILE_ROWS
                vbuf[ch, start:start + TILE_ROWS, lanes] = v

            spread([wbuf[j, ch, :, i * 128:i * 128 + 128] for i in range(reps)], share, put)
            return carry

        lax.fori_loop(0, 2, unit, 0)

    def send_edge(j):
        down = up if j == 0 else jnp.logical_not(up)
        row8 = lax.broadcasted_iota(jnp.int32, (8, width), 0)
        block = []
        for ch in range(2):
            sums, ours = edge[j, ch], jnp.where(down, strip[3, ch], strip[0, ch])
            below = jnp.where(down, ours, sums)
            above = jnp.where(down, sums, ours)
            block.append(jnp.where(row8 < 4, below, above))
        sblk[j] = jnp.concatenate(block, axis=0).astype(BF16)
        offset = jnp.where(down, 1, -1)
        lands = jnp.where(down, 0, 1)
        send(sblk.at[j], rblk.at[lands], blk_s.at[j], blk_r.at[lands], at(offset))

    for m in range(4):
        for k in range(2):
            weigh(m, k)

    @pl.when(jnp.logical_and(early, outer))
    def _():
        pl.semaphore_wait(go_sem, crossing)
        for e, offset in enumerate(NEAR):
            @pl.when(crosses(offset))
            def _():
                send_meta(e).start()
        send_far()

        @pl.when(next_crosses)
        def _():
            send_next()

    @pl.when(jnp.logical_and(early, inner))
    def _():
        pl.semaphore_wait(go_sem, 1)
        forward()

    send_edge(0)
    for m in range(4, GROUPS):
        take_meta(m)
    positions, gains = pos_all[...], gain_all[...]
    for j in range(12):
        own = jnp.where(positions == positions[j:j + 1], gains, 0.0)
        g_all[j:j + 1] = jnp.sum(own, axis=0, keepdims=True)
    for m in range(GROUPS):
        place(m)
    for m in range(4):
        for k in range(2):
            filter_columns(m, k)

    per_channel = width // SPAN

    def chunk(n):
        return n // per_channel, pl.ds(pl.multiple_of(lax.rem(n, per_channel) * SPAN, SPAN), SPAN)

    def nearer(n, carry):
        ch, cols = chunk(n)
        acc[ch, :, cols] = jnp.dot(
            mbuf[:, 0:NEARER], vbuf[ch, 0:NEARER, cols], preferred_element_type=F32
        )
        return carry

    lax.fori_loop(0, 2 * per_channel, nearer, 0)

    for k in range(2):
        for m in range(4, GROUPS):
            weigh(m, k)
        if k == 1:
            send_edge(1)
        for m in range(4, GROUPS):
            filter_columns(m, k)

    def farther(n, carry):
        ch, cols = chunk(n)
        made = acc[ch, :, cols] + jnp.dot(
            mbuf[:, NEARER:], vbuf[ch, NEARER:, cols], preferred_element_type=F32
        )
        out_ref[0, ch, :, cols] = made.astype(BF16)
        rim[ch, 0:16, cols] = made[0:16]
        rim[ch, 16:32, cols] = made[OWNER_ROWS - 16:]
        return carry

    lax.fori_loop(0, 2 * per_channel, farther, 0)

    for j in range(2):
        remote(sblk.at[j], rblk.at[j], blk_s.at[j], blk_r.at[j], at(1)).wait_recv()
    row_in = lax.rem(row16, 8)
    ramp_rim = jnp.minimum(row_in + 1, 8 - row_in).astype(F32)
    inside = jnp.where(
        row_in < 4, jnp.where(me == n_tile - 1, 0.0, 1.0).astype(F32), jnp.where(me == 0, 0.0, 1.0).astype(F32)
    )
    inside = jnp.where(jnp.logical_or(row_in == 3, row_in == 4), 0.0, inside)
    beside_rows = []
    for i in range(reps):
        lanes = slice(i * 128, i * 128 + 128)
        below = jnp.concatenate([strip[2, 0, :, lanes], strip[2, 1, :, lanes]], axis=0)
        above = jnp.concatenate([strip[1, 0, :, lanes], strip[1, 1, :, lanes]], axis=0)
        rows = rblk[0, :, lanes].astype(F32) + rblk[1, :, lanes].astype(F32) + jnp.where(row_in < 4, below, above)
        if i == 0:
            weights = jnp.where(row_in < 4, rows[3:4], rows[4:5]) * ramp_rim
        beside_rows.append(rows.astype(BF16))
    rim_share = inside / jnp.maximum(weights, 1.0)

    def put_rim(d, lanes, v):
        vrim[d * TILE_ROWS:(d + 1) * TILE_ROWS, lanes] = v

    spread(beside_rows, rim_share, put_rim)
    for ch in range(2):
        for first in range(0, width, SPAN):
            cols = slice(first, first + SPAN)
            made = rim[ch, :, cols] + jnp.dot(mrim[ch], vrim[:, cols], preferred_element_type=F32)
            out_ref[0, ch, 0:16, cols] = made[0:16].astype(BF16)
            out_ref[0, ch, OWNER_ROWS - 16:, cols] = made[16:32].astype(BF16)

    for e in range(4):
        for k in range(2):
            send_tile(e, k, NEAR[e]).wait_send()
    for e in range(5):
        send_meta(e).wait_send()
    for copy in sends:
        copy.wait_send()

    @pl.when(inner)
    def _():
        for k in range(1, n_plane):
            remote(prof.at[core, plane], prof.at[core, plane], gat_s.at[k], gat_r.at[plane], mate(k)).wait_send()
        to_side.wait_send()
        pass_on.wait_send()


def solution(mesh):
    n_tile, n_plane = mesh.shape["tile"], mesh.shape["plane"]

    def per_device(raw_tiles, flat_profile, dark_profile, destinations, positions, levels):
        width = raw_tiles.shape[-1]
        tile = (2, TILE_ROWS, width)
        dma = pltpu.SemaphoreType.DMA
        return pl.pallas_call(
            functools.partial(stitch_kernel, n_tile, n_plane, width),
            out_shape=pltpu.VMEM((1, 2, OWNER_ROWS, width), BF16),
            in_specs=[pl.BlockSpec(memory_space=pltpu.HBM)] * 6,
            out_specs=pl.BlockSpec(memory_space=pltpu.VMEM),
            scratch_shapes=[
                pltpu.SMEM((1, 8), jnp.int32),
                pltpu.SMEM((1, 8), jnp.int32),
                pltpu.SMEM((1, 8), jnp.int32),
                pltpu.VMEM((8,) + tile, BF16),
                pltpu.VMEM((5, 2) + tile, BF16),
                pltpu.VMEM((6, 2) + tile, BF16),
                pltpu.VMEM((6, 8, 128), F32),
                pltpu.VMEM((6, 8, 128), F32),
                pltpu.VMEM((2, n_plane, 2, TILE_ROWS // n_plane, width), BF16),
                pltpu.VMEM(tile, F32),
                pltpu.VMEM(tile, F32),
                pltpu.VMEM((16, 128), F32),
                pltpu.VMEM((16, 128), F32),
                pltpu.VMEM((16, 128), F32),
                pltpu.VMEM((2, 2, 8, width), F32),
                pltpu.VMEM((4, 2, 8, width), F32),
                pltpu.VMEM((2, 16, width), BF16),
                pltpu.VMEM((2, 16, width), BF16),
                pltpu.VMEM(tile, BF16),
                pltpu.VMEM((12,) + tile, BF16),
                pltpu.VMEM((2, DEPTH, width), BF16),
                pltpu.VMEM((OWNER_ROWS, DEPTH), BF16),
                pltpu.VMEM((2, OWNER_ROWS, width), F32),
                pltpu.VMEM((2, 32, width), F32),
                pltpu.VMEM((64, width), BF16),
                pltpu.VMEM((2, 32, 64), BF16),
                dma, dma, dma((3,)), pltpu.SemaphoreType.REGULAR,
                dma((5, 2)), dma((5, 2)), dma((5,)), dma((5,)),
                dma((n_plane,)), dma((n_plane,)), dma, dma, dma, dma,
                dma((2,)), dma((2,)), dma, dma,
            ],
            compiler_params=pltpu.CompilerParams(
                collective_id=0, has_side_effects=True, vmem_limit_bytes=(62 << 20) - (64 << 10)
            ),
            name="stitch",
        )(destinations[:, :, 0], positions, levels, raw_tiles, flat_profile, dark_profile)

    placed = (
        P("plane", "tile", None, None, None),
        P(None, "plane", None),
        P(None, "plane", None),
        P("plane", "tile", None),
        P("plane", "tile"),
        P("plane", "tile"),
    )
    return jax.shard_map(
        per_device, mesh=mesh, in_specs=placed, out_specs=P("plane", None, "tile", None), check_vma=False
    )
```

time: 34.6 us -> 30.6 us (0.88)
  the two profiles are of different devices: /device:TPU:32 before, /device:TPU:192 now
where the time goes in v3:
time: 30.6 us; the launch traced here: 30.5 us
  Pallas kernels  29.2 us (95%)
  local copies, waits for them, and re-layouts  1.32 us (4%)
    pallas_call x1, Pallas kernels, per_device(): pl.pallas_call(functools.partial(stitch_kernel, n_tile, n_plane, width),...  29.2 us
    unnamed x1, local copies, waits for them, and re-layouts  1.32 us

profile of v3, /device:TPU:192, one launch (start us, length us, event | category | flops | bytes accessed | tf_op | source)
XLA Modules:
  0.0 30.5 jit_solution(9583875581650468393)
XLA Ops:
  0.0 29.2 %stitch.1 = bf16[1,2,512,1024]{3,2,1,0:T(8,128)(2,1)S(1)} custom-call(s32[1,8]{1,0:T(1,128)} %bitcast.1, s32[1,8]{1,0:T(1,128)} %pos_hbm.1, s32[1,8]{1,0:T(1,128)} %level_hbm.1, bf16[1,8,2,16,1024]{4,3,2,1,0:T(8,128)(2,1)} %raw_ref.1, bf16[2,4,1024]{2,1,0:T(4,128)(2,1)} %flat_ref.1, bf16[2,4,1024]{2,1,0:T(4,128)(2,1)} %dark_ref.1), custom_call_target="tpu_custom_call" | custom-call | tf_op jit(solution)/shard_map/stitch/pallas_call | solution.py:519
  29.2 1.3 %copy.8 = bf16[1,2,512,1024]{3,2,1,0:T(8,128)(2,1)} copy(bf16[1,2,512,1024]{3,2,1,0:T(8,128)(2,1)S(1)} %stitch.1) | data formatting | bytes 4194304

commit v4 on v3

--- a/solution.py
+++ b/solution.py
@@ -225,6 +225,24 @@
         send_next()
         send_near()
 
+    @pl.when(jnp.logical_and(early, outer))
+    def _():
+        pl.semaphore_wait(go_sem, crossing)
+        for e, offset in enumerate(NEAR):
+            @pl.when(crosses(offset))
+            def _():
+                send_meta(e).start()
+        send_far()
+
+        @pl.when(next_crosses)
+        def _():
+            send_next()
+
+    @pl.when(jnp.logical_and(early, inner))
+    def _():
+        pl.semaphore_wait(go_sem, 1)
+        forward()
+
     @pl.when(jnp.logical_not(inner))
     def _():
         to_side.wait_recv()
@@ -397,24 +415,6 @@
     for m in range(4):
         for k in range(2):
             weigh(m, k)
-
-    @pl.when(jnp.logical_and(early, outer))
-    def _():
-        pl.semaphore_wait(go_sem, crossing)
-        for e, offset in enumerate(NEAR):
-            @pl.when(crosses(offset))
-            def _():
-                send_meta(e).start()
-        send_far()
-
-        @pl.when(next_crosses)
-        def _():
-            send_next()
-
-    @pl.when(jnp.logical_and(early, inner))
-    def _():
-        pl.semaphore_wait(go_sem, 1)
-        forward()
 
     send_edge(0)
     for m in range(4, GROUPS):

time: 30.6 us -> 27.9 us (0.912)
  the two profiles are of different devices: /device:TPU:192 before, /device:TPU:1 now
where the time goes in v4:
time: 27.9 us; the launch traced here: 27.8 us
  Pallas kernels  26.5 us (95%)
  local copies, waits for them, and re-layouts  1.32 us (5%)
    pallas_call x1, Pallas kernels, per_device(): pl.pallas_call(functools.partial(stitch_kernel, n_tile, n_plane, width),...  26.5 us
    unnamed x1, local copies, waits for them, and re-layouts  1.32 us

profile of v4, /device:TPU:1, one launch (start us, length us, event | category | flops | bytes accessed | tf_op | source)
XLA Modules:
  0.0 27.8 jit_solution(9997860543125079879)
XLA Ops:
  0.0 26.5 %stitch.1 = bf16[1,2,512,1024]{3,2,1,0:T(8,128)(2,1)S(1)} custom-call(s32[1,8]{1,0:T(1,128)} %bitcast.1, s32[1,8]{1,0:T(1,128)} %pos_hbm.1, s32[1,8]{1,0:T(1,128)} %level_hbm.1, bf16[1,8,2,16,1024]{4,3,2,1,0:T(8,128)(2,1)} %raw_ref.1, bf16[2,4,1024]{2,1,0:T(4,128)(2,1)} %flat_ref.1, bf16[2,4,1024]{2,1,0:T(4,128)(2,1)} %dark_ref.1), custom_call_target="tpu_custom_call" | custom-call | tf_op jit(solution)/shard_map/stitch/pallas_call | solution.py:519
  26.5 1.3 %copy.8 = bf16[1,2,512,1024]{3,2,1,0:T(8,128)(2,1)} copy(bf16[1,2,512,1024]{3,2,1,0:T(8,128)(2,1)S(1)} %stitch.1) | data formatting | bytes 4194304

commit v5 on v4

--- a/solution.py
+++ b/solution.py
@@ -189,13 +189,13 @@
     def _():
         remote(sbuf.at[far, 1], passing, tile_s.at[far, 1], pass_r, at(-far_offset)).start()
 
+    @pl.when(jnp.logical_and(outer, jnp.logical_or(late, jnp.logical_not(next_crosses))))
+    def _():
+        send_next()
+
     @pl.when(jnp.logical_and(outer, late))
     def _():
         send_far()
-
-    @pl.when(jnp.logical_and(outer, jnp.logical_or(late, jnp.logical_not(next_crosses))))
-    def _():
-        send_next()
 
     for k in range(2):
         send(sbuf.at[4, k], rbuf.at[4, k], tile_s.at[4, k], tile_r.at[4, k], at(half))
@@ -210,6 +210,12 @@
         remote(sbuf.at[far, 1], passing, tile_s.at[far, 1], pass_r, at(-far_offset)).wait_recv()
         pass_on.start()
 
+    @pl.when(inner)
+    def _():
+        send_tile(far, 1, far_offset).start()
+        send_far()
+        send_next()
+
     @pl.when(jnp.logical_and(inner, late))
     def _():
         forward()
@@ -220,9 +226,6 @@
             source = lax.rem(plane + k, n_plane)
             remote(prof.at[core, source], prof.at[core, source], gat_s.at[k], gat_r.at[source], mate(k)).wait_recv()
         to_side.start()
-        send_tile(far, 1, far_offset).start()
-        send_far()
-        send_next()
         send_near()
 
     @pl.when(jnp.logical_and(early, outer))
@@ -232,11 +235,12 @@
             @pl.when(crosses(offset))
             def _():
                 send_meta(e).start()
-        send_far()
 
         @pl.when(next_crosses)
         def _():
             send_next()
+
+        send_far()
 
     @pl.when(jnp.logical_and(early, inner))
     def _():
@@ -396,7 +400,7 @@
             spread([wbuf[j, ch, :, i * 128:i * 128 + 128] for i in range(reps)], share, put)
             return carry
 
-        lax.fori_loop(0, 2, unit, 0)
+        lax.fori_loop(0, 2, unit, 0, unroll=True)
 
     def send_edge(j):
         down = up if j == 0 else jnp.logical_not(up)
@@ -413,6 +417,8 @@
         send(sblk.at[j], rblk.at[lands], blk_s.at[j], blk_r.at[lands], at(offset))
 
     for m in range(4):
+        place(m)
+    for m in range(4):
         for k in range(2):
             weigh(m, k)
 
@@ -423,7 +429,7 @@
     for j in range(12):
         own = jnp.where(positions == positions[j:j + 1], gains, 0.0)
         g_all[j:j + 1] = jnp.sum(own, axis=0, keepdims=True)
-    for m in range(GROUPS):
+    for m in range(4, GROUPS):
         place(m)
     for m in range(4):
         for k in range(2):
@@ -434,28 +440,18 @@
     def chunk(n):
         return n // per_channel, pl.ds(pl.multiple_of(lax.rem(n, per_channel) * SPAN, SPAN), SPAN)
 
-    def nearer(n, carry):
-        ch, cols = chunk(n)
-        acc[ch, :, cols] = jnp.dot(
-            mbuf[:, 0:NEARER], vbuf[ch, 0:NEARER, cols], preferred_element_type=F32
-        )
-        return carry
-
-    lax.fori_loop(0, 2 * per_channel, nearer, 0)
 
     for k in range(2):
         for m in range(4, GROUPS):
             weigh(m, k)
-        if k == 1:
-            send_edge(1)
+    send_edge(1)
+    for k in range(2):
         for m in range(4, GROUPS):
             filter_columns(m, k)
 
     def farther(n, carry):
         ch, cols = chunk(n)
-        made = acc[ch, :, cols] + jnp.dot(
-            mbuf[:, NEARER:], vbuf[ch, NEARER:, cols], preferred_element_type=F32
-        )
+        made = jnp.dot(mbuf[...], vbuf[ch, :, cols], preferred_element_type=F32)
         out_ref[0, ch, :, cols] = made.astype(BF16)
         rim[ch, 0:16, cols] = made[0:16]
         rim[ch, 16:32, cols] = made[OWNER_ROWS - 16:]

time: 27.9 us -> 26.9 us (0.964)
  the two profiles are of different devices: /device:TPU:1 before, /device:TPU:0 now
where the time goes in v5:
time: 26.9 us; the launch traced here: 26.8 us
  Pallas kernels  25.5 us (95%)
  local copies, waits for them, and re-layouts  1.32 us (5%)
    pallas_call x1, Pallas kernels, per_device(): pl.pallas_call(functools.partial(stitch_kernel, n_tile, n_plane, width),...  25.5 us
    unnamed x1, local copies, waits for them, and re-layouts  1.32 us

profile of v5, /device:TPU:0, one launch (start us, length us, event | category | flops | bytes accessed | tf_op | source)
XLA Modules:
  0.0 26.8 jit_solution(5848728492418108122)
XLA Ops:
  0.0 25.5 %stitch.1 = bf16[1,2,512,1024]{3,2,1,0:T(8,128)(2,1)S(1)} custom-call(s32[1,8]{1,0:T(1,128)} %bitcast.1, s32[1,8]{1,0:T(1,128)} %pos_hbm.1, s32[1,8]{1,0:T(1,128)} %level_hbm.1, bf16[1,8,2,16,1024]{4,3,2,1,0:T(8,128)(2,1)} %raw_ref.1, bf16[2,4,1024]{2,1,0:T(4,128)(2,1)} %flat_ref.1, bf16[2,4,1024]{2,1,0:T(4,128)(2,1)} %dark_ref.1), custom_call_target="tpu_custom_call" | custom-call | tf_op jit(solution)/shard_map/stitch/pallas_call | solution.py:515
  25.5 1.3 %copy.8 = bf16[1,2,512,1024]{3,2,1,0:T(8,128)(2,1)} copy(bf16[1,2,512,1024]{3,2,1,0:T(8,128)(2,1)S(1)} %stitch.1) | data formatting | bytes 4194304
